TPU v7x, 512 devices: a whole 4x4x16 slice. The times are simulated.
512 devices in a mesh: dp: 64 (over y_hi, z, core), layer: 8 (over x, y_lo).
Axes of the slice: x: 4, y: 4 (y_hi: 2, y_lo: 2; y = y_hi * 2 + y_lo), z: 16, core: 2. Of those that a mesh axis runs over, the one named last changes fastest.
Arguments:
- query_inputs: bfloat16 [8, 64, 128, 4096], P('layer', 'dp'), may hold values from -6 to 6
- query_cotangents: bfloat16 [8, 64, 128, 4096], P('layer', 'dp'), may hold values from -6 to 6
- query_lengths: int32 [64], P('dp'), may hold values from 64 to 128, as said below
- proj_in: bfloat16 [8, 64, 4096], P('layer'), may hold values from -0.09375 to 0.09375
- proj_out: bfloat16 [8, 64, 4096], P('layer'), may hold values from -0.09375 to 0.09375
- out_factor: float32 [8, 64, 64], P('layer'), may hold values from -1 to 5, as said below
- in_factor: float32 [8, 64, 64], P('layer'), may hold values from -1 to 5, as said below
- train_grads: bfloat16 [8, 8192, 4096], P('layer', 'dp'), may hold values from -0.0009765625 to 0.0009765625
Outputs:
- scores: float32 [64, 8192], P('layer', 'dp')
Inputs may be any that keep to these rules, and one draw needn't show every extreme that they name: `query_lengths`: some query sequence has 128 valid tokens and some has 64. `out_factor`: each matrix is symmetric positive definite. `in_factor`: each matrix is symmetric positive definite.
All inputs are finite; a program needn't handle non-finite values.
Results may differ from a plain program's by a relative error of at most 0.0057.
Values may be sent and summed in bfloat16 or wider, within the bound.
No kernel may reach another device: no remote copies, remote signals or barrier semaphores. Data moves between devices by JAX's collectives and lax.ppermute only.
A program may use at most 64 MiB of HBM per device.

v0:
```python
import jax
import jax.numpy as jnp
from jax import lax
from jax.sharding import PartitionSpec as P


def body(
    query_inputs,
    query_cotangents,
    query_lengths,
    proj_in,
    proj_out,
    out_factor,
    in_factor,
    train_grads,
):
    blocks, queries, length, width = query_inputs.shape
    factor_rank = proj_in.shape[1]
    slots = lax.broadcasted_iota(jnp.int32, (1, queries, length, 1), 2)
    valid = slots < query_lengths[None, :, None, None]
    out_side = jnp.einsum(
        "bqld,brd->bqlr", query_cotangents, proj_out, preferred_element_type=jnp.float32
    )
    out_side = jnp.where(valid, out_side, 0.0).astype(jnp.bfloat16)
    in_side = jnp.einsum(
        "bqld,brd->bqlr", query_inputs, proj_in, preferred_element_type=jnp.float32
    ).astype(jnp.bfloat16)
    query_gradient_rows = jnp.einsum(
        "bqlr,bqls->bqrs", out_side, in_side, preferred_element_type=jnp.float32
    ).astype(jnp.bfloat16)
    flat_query = query_gradient_rows.reshape(blocks, queries, factor_rank * factor_rank)
    flat_grads = lax.all_gather(flat_query, "dp", axis=1, tiled=True)
    row_count = flat_grads.shape[1]
    widened = flat_grads.reshape(blocks, row_count, factor_rank, factor_rank).astype(jnp.float32)
    left_projection = jnp.einsum(
        "brk,bnks->bnrs", out_factor, widened, precision=lax.Precision.HIGHEST
    )
    both_sides = jnp.einsum(
        "bnrs,bst->bnrt", left_projection, in_factor, precision=lax.Precision.HIGHEST
    )
    partial_scores = jnp.einsum(
        "bnk,btk->nt",
        both_sides.astype(jnp.bfloat16).reshape(blocks, row_count, factor_rank * factor_rank),
        train_grads,
        preferred_element_type=jnp.float32,
    )
    return lax.psum_scatter(partial_scores, "layer", scatter_dimension=0, tiled=True)


def solution(mesh):
    in_specs = (
        P("layer", "dp", None, None),
        P("layer", "dp", None, None),
        P("dp"),
        P("layer", None, None),
        P("layer", None, None),
        P("layer", None, None),
        P("layer", None, None),
        P("layer", "dp", None),
    )
    out_specs = P("layer", "dp")
    return jax.shard_map(body, mesh=mesh, in_specs=in_specs, out_specs=out_specs, check_vma=False)
```

profile of v0, /device:TPU:16, one launch (start us, length us, event | category | flops | bytes accessed | tf_op | source)
XLA Modules:
  0.0 137.2 jit_solution(3294647582231593222)
XLA Ops:
  0.0 0.0 copy-start
  0.8 0.5 copy-done
  1.2 1.5 %fusion.5 = bf16[128,64]{0,1:T(8,128)(2,1)S(1)} fusion(bf16[1,1,128,4096]{3,2,1,0:T(8,128)(2,1)S(1)} %copy-done, bf16[1,64,4096]{2,1,0:T(8,128)(2,1)} %param.12, pred[128]{0:T(512)(128)(4,1)S(1)} %iota_compare_fusion), kind=kOutput, calls=%fused_computation.5 | convolution fusion | flops 67125248 | bytes 1589376 | tf_op jit(solution)/shard_map/bqld,brd->bqlr/dot_general | solution.py:21
  2.8 2.0 %convolution_convert_fusion.1 = bf16[64,64]{1,0:T(8,128)(2,1)S(1)} fusion(bf16[128,64]{0,1:T(8,128)(2,1)S(1)} %fusion.5, bf16[1,1,128,4096]{3,2,1,0:T(8,128)(2,1)} %param.8, bf16[1,64,4096]{2,1,0:T(8,128)(2,1)} %param.11), kind=kOutput, calls=%fused_computation.6 | convolution fusion | flops 68169728 | bytes 1597440 | tf_op jit(solution)/shard_map/bqlr,bqls->bqrs/dot_general | solution.py:28
  4.7 0.1 reshape.67
  4.8 0.0 copy-start.1
  4.8 83.4 %all_gather.3 = bf16[1,64,4096]{2,0,1:T(2,128)(2,1)S(1)} all-gather(bf16[1,1,4096]{2,0,1:T(2,128)(2,1)S(1)} %bitcast.41), channel_id=1, replica_groups=mesh['dp'=64,'layer'=8] {'dp'}, dimensions={1}, use_global_device_ids=true | all-gather | bytes 532480 | tf_op jit(solution)/shard_map/all_gather | solution.py:32
  88.2 3.1 %reduce = bf16[64,4096]{1,0:T(8,128)(2,1)S(1)} reduce(bf16[1,64,4096]{2,0,1:T(2,128)(2,1)S(1)} %all_gather.3, bf16[]{:T(256)} %constant.14), dimensions={0}, to_apply=%all_gather.3.reduce_sub_computation | reduce | bytes 1048578 | tf_op jit(solution)/shard_map/all_gather | solution.py:32
  91.3 0.0 copy-start.2
  91.4 1.1 reshape.68
  92.5 0.0 copy-done.1
  92.5 1.2 fusion.15
  93.7 0.0 copy-done.2
  93.7 3.5 %fusion.2 = bf16[64,64,64]{2,1,0:T(8,128)(2,1)S(1)} fusion(f32[64,64,64]{2,1,0:T(8,128)S(1)} %fusion.15, f32[1,64,64]{2,1,0:T(8,128)S(1)} %copy-done.2), kind=kOutput, calls=%fused_computation.2 | convolution fusion | flops 201588736 | bytes 1589248 | tf_op jit(solution)/shard_map/bnrs,bst->bnrt/dot_general | solution.py:38
  97.3 0.8 reshape.72
  98.1 1.7 %fusion.6 = f32[64,128]{1,0:T(8,128)S(1)} fusion(bf16[64,4096]{1,0:T(8,128)(2,1)S(1)} %reshape.72, bf16[1,128,4096]{2,1,0:T(8,128)(2,1)} %param.15), kind=kOutput, calls=%fused_computation.7 | convolution fusion | flops 67108864 | bytes 1605632 | tf_op jit(solution)/shard_map/bnk,btk->nt/dot_general | solution.py:41
  99.8 34.9 %all-reduce = f32[64,128]{1,0:T(8,128)S(1)} all-reduce(f32[64,128]{1,0:T(8,128)S(1)} %fusion.6), channel_id=2, replica_groups=mesh['dp'=64,'layer'=8] {'layer'}, use_global_device_ids=true, to_apply=%region_0.1.clone | all-reduce | flops 8192 | bytes 65536
  134.7 1.3 dynamic-slice
  136.6 0.6 constant_dynamic-slice_fusion
  (1 shorter events, 0.0 us)
Async XLA Ops:
  0.0 1.2 copy-start
  4.8 87.7 %copy-start.1 = (f32[1,64,64]{2,1,0:T(8,128)S(1)}, f32[1,64,64]{2,1,0:T(8,128)}, u32[]{:S(2)}) copy-start(f32[1,64,64]{2,1,0:T(8,128)} %param.13) | copy-start | bytes 49156
  91.3 2.4 %copy-start.2 = (f32[1,64,64]{2,1,0:T(8,128)S(1)}, f32[1,64,64]{2,1,0:T(8,128)}, u32[]{:S(2)}) copy-start(f32[1,64,64]{2,1,0:T(8,128)} %param.14) | copy-start | bytes 49156
where the time goes:
time: 138 us; the launch traced here: 137 us
  blocking collectives  118 us (86%)
  matrix products  9.94 us (7%)
  local copies, waits for them, and re-layouts  4.39 us (3%)
  other arithmetic  3.15 us (2%)
  between operations  1.48 us (1%)
    all_gather x1, blocking collectives, body(): flat_grads = lax.all_gather(flat_query, 'dp', axis=1, tiled=True)  83.4 us
    unnamed x1, blocking collectives  34.9 us
    dot_general x1, matrix products, body(): jnp.einsum('bnrs,bst->bnrt', left_projection, in_factor, precision=lax.Pr...  3.53 us
    all_gather x1, other arithmetic, body(): flat_grads = lax.all_gather(flat_query, 'dp', axis=1, tiled=True)  3.15 us

commit v1 on v0

v1 whole, which is shorter than its diff:
```python
import jax
import jax.numpy as jnp
from jax import lax
from jax.sharding import Mesh, PartitionSpec as P

CORES = 2
Y_HI = 2
Y_LO = 2


def body(
    query_inputs,
    query_cotangents,
    query_lengths,
    proj_in,
    proj_out,
    out_factor,
    in_factor,
    train_grads,
):
    length = query_inputs.shape[2]
    rank = proj_in.shape[1]
    flat = rank * rank
    slots = lax.broadcasted_iota(jnp.int32, (length, 1), 0)
    out_side = jnp.einsum(
        "ld,rd->lr", query_cotangents[0, 0], proj_out[0], preferred_element_type=jnp.float32
    )
    out_side = jnp.where(slots < query_lengths[0], out_side, 0.0).astype(jnp.bfloat16)
    in_side = jnp.einsum(
        "ld,rd->lr", query_inputs[0, 0], proj_in[0], preferred_element_type=jnp.float32
    ).astype(jnp.bfloat16)
    grad = jnp.einsum("lr,ls->rs", out_side, in_side, preferred_element_type=jnp.float32)
    grad = grad.astype(jnp.bfloat16).astype(jnp.float32)
    left = jnp.dot(out_factor[0], grad, precision=lax.Precision.HIGHEST)
    conditioned = jnp.dot(left, in_factor[0], precision=lax.Precision.HIGHEST)
    conditioned = conditioned.astype(jnp.bfloat16).reshape(flat // 128, 128)

    places = lax.axis_size(("yh", "z"))
    sent = jnp.broadcast_to(conditioned[None], (places, flat // 128, 128))
    mine = lax.all_to_all(sent, ("yh", "z"), 0, 0)
    swap = [(i, CORES - 1 - i) for i in range(CORES)]
    other = lax.ppermute(mine, "core", swap)
    first = lax.axis_index("core") == 0
    even = jnp.where(first, mine, other)
    odd = jnp.where(first, other, mine)
    queries = jnp.stack([even, odd], axis=1).reshape(places * CORES, flat)

    partial = lax.dot_general(
        queries, train_grads[0], (((1,), (1,)), ((), ())), preferred_element_type=jnp.float32
    )
    layers = lax.axis_size(("x", "yl"))
    terms = lax.all_to_all(
        partial.reshape(layers, -1, partial.shape[1]), ("x", "yl"), 0, 0
    )
    return jnp.sum(terms, axis=0)


def solution(mesh):
    dp, layer = mesh.devices.shape
    shape = (Y_HI, dp // (Y_HI * CORES), CORES, layer // Y_LO, Y_LO)
    fine = Mesh(mesh.devices.reshape(shape), ("yh", "z", "core", "x", "yl"))
    dp, layer = ("yh", "z", "core"), ("x", "yl")
    in_specs = (
        P(layer, dp, None, None),
        P(layer, dp, None, None),
        P(dp),
        P(layer, None, None),
        P(layer, None, None),
        P(layer, None, None),
        P(layer, None, None),
        P(layer, dp, None),
    )
    return jax.shard_map(
        body, mesh=fine, in_specs=in_specs, out_specs=P(layer, dp), check_vma=False
    )
```

time: 138 us -> 62.6 us (0.45)
  the two profiles are of different devices: /device:TPU:16 before, /device:TPU:1 now
where the time goes in v1:
time: 62.6 us; the launch traced here: 62.2 us
  blocking collectives  49 us (78%)
  starting transfers between devices  5.09 us (8%)
  matrix products  3.02 us (5%)
  local copies, waits for them, and re-layouts  2.41 us (4%)
  waiting for transfers between devices  1.13 us (2%)
  between operations  0.91 us (1%)
  other arithmetic  0.72 us (1%)
    all_to_all x1, blocking collectives, body(): mine = lax.all_to_all(sent, ('yh', 'z'), 0, 0)  40 us
    all_to_all x1, blocking collectives, body(): lax.all_to_all(partial.reshape(layers, -1, partial.shape[1]), ('x', 'yl')...  9 us
    ppermute x1, starting transfers between devices, body(): other = lax.ppermute(mine, 'core', swap)  5.09 us
    unnamed x12, local copies, waits for them, and re-layouts  2.06 us
    dot_general x1, matrix products, body(): jnp.einsum('ld,rd->lr', query_inputs[0, 0], proj_in[0], preferred_element...  1.52 us
  transfers between devices with their start and end apart: 1, of which 1 were waited for; matrix products, arithmetic and copies ran while one was open for 0% of the time, Pallas kernels for 0%

profile of v1, /device:TPU:1, one launch (start us, length us, event | category | flops | bytes accessed | tf_op | source)
XLA Modules:
  0.0 62.2 jit_solution(9459384679370758417)
XLA Ops:
  0.0 0.0 copy-start
  0.0 0.0 copy-start.1
  0.8 0.4 copy-done
  1.2 0.0 copy-start.3
  1.2 1.5 %convolution_convert_fusion = bf16[128,64]{1,0:T(8,128)(2,1)S(1)} fusion(bf16[1,1,128,4096]{3,2,1,0:T(8,128)(2,1)S(1)} %copy-done, bf16[1,64,4096]{2,1,0:T(8,128)(2,1)} %param.11), kind=kOutput, calls=%fused_computation.1 | convolution fusion | flops 67117056 | bytes 1589248 | tf_op jit(solution)/shard_map/ld,rd->lr/dot_general | solution.py:29
  2.8 0.0 copy-done.1
  2.8 0.0 copy-done.3
  2.8 0.0 copy-start.4
  2.8 0.6 fusion.2
  3.4 0.2 copy-done.4
  3.5 0.0 copy-start.5
  3.6 0.2 fusion.12
  3.8 0.5 copy-done.5
  4.3 0.2 convolution_convert_fusion.1
  4.6 0.1 broadcast_in_dim.21
  4.7 40.0 %all_to_all.10 = bf16[32,32,128]{2,1,0:T(8,128)(2,1)S(1)} all-to-all(bf16[32,32,128]{2,1,0:T(8,128)(2,1)S(1)} %broadcast_in_dim.22), channel_id=1, replica_groups=mesh['yh'=2,'z'=16,'core'=2,'x'=4,'yl'=2] {'yh','z'}, dimensions={0} | all-to-all | bytes 524288 | tf_op jit(solution)/shard_map/all_to_all | solution.py:40
  44.6 5.1 %collective-permute-start = (bf16[32,32,128]{2,1,0:T(8,128)(2,1)S(1)}, bf16[32,32,128]{2,1,0:T(8,128)(2,1)S(1)}, u32[]{:S(2)}, u32[]{:S(2)}) collective-permute-start(bf16[32,32,128]{2,1,0:T(8,128)(2,1)S(1)} %all_to_all.10), channel_id=1, source_target_pairs={{0,8},{8,0},{1,9},{9,1},{2,10},{10,2},{3,11},{11,3},{4,12},{12,4},... | collective-permute-start | bytes 786440 | tf_op jit(solution)/shard_map/ppermute | solution.py:42
  49.7 1.1 %collective-permute-done = bf16[32,32,128]{2,1,0:T(8,128)(2,1)S(1)} collective-permute-done((bf16[32,32,128]{2,1,0:T(8,128)(2,1)S(1)}, bf16[32,32,128]{2,1,0:T(8,128)(2,1)S(1)}, u32[]{:S(2)}, u32[]{:S(2)}) %collective-permute-start) | collective-permute-done | bytes 262176 | tf_op jit(solution)/shard_map/ppermute | solution.py:42
  50.9 0.0 copy-start.2
  50.9 0.1 pad_maximum_fusion
  51.0 0.2 dot_general.25
  51.2 0.9 %copy-done.2 = bf16[1,128,4096]{2,1,0:T(8,128)(2,1)S(1)} copy-done((bf16[1,128,4096]{2,1,0:T(8,128)(2,1)S(1)}, bf16[1,128,4096]{2,1,0:T(8,128)(2,1)}, u32[]{:S(2)}) %copy-start.2) | copy-done | bytes 1048600
  52.2 0.5 fusion.3
  52.6 9.0 %all_to_all.11 = f32[8,8,128]{2,1,0:T(8,128)S(1)} all-to-all(f32[8,8,128]{2,1,0:T(8,128)S(1)} %fusion.3), channel_id=1, replica_groups=mesh['yh'=2,'z'=16,'core'=2,'x'=4,'yl'=2] {'x','yl'}, dimensions={0} | all-to-all | bytes 65536 | tf_op jit(solution)/shard_map/all_to_all | solution.py:52
  61.6 0.6 reduce_sum.9
  (3 shorter events, 0.1 us)
Async XLA Ops:
  0.0 1.2 %copy-start = (bf16[1,1,128,4096]{3,2,1,0:T(8,128)(2,1)S(1)}, bf16[1,1,128,4096]{3,2,1,0:T(8,128)(2,1)}, u32[]{:S(2)}) copy-start(bf16[1,1,128,4096]{3,2,1,0:T(8,128)(2,1)} %param.8) | copy-start | bytes 3145732
  0.0 2.8 %copy-start.1 = (bf16[1,1,128,4096]{3,2,1,0:T(8,128)(2,1)S(1)}, bf16[1,1,128,4096]{3,2,1,0:T(8,128)(2,1)}, u32[]{:S(2)}) copy-start(bf16[1,1,128,4096]{3,2,1,0:T(8,128)(2,1)} %param.9) | copy-start | bytes 3145732
  1.2 1.5 %copy-start.3 = (bf16[1,64,4096]{2,1,0:T(8,128)(2,1)S(1)}, bf16[1,64,4096]{2,1,0:T(8,128)(2,1)}, u32[]{:S(2)}) copy-start(bf16[1,64,4096]{2,1,0:T(8,128)(2,1)} %param.12) | copy-start | bytes 1572868
  2.8 0.8 %copy-start.4 = (f32[1,64,64]{2,1,0:T(8,128)S(1)}, f32[1,64,64]{2,1,0:T(8,128)}, u32[]{:S(2)}) copy-start(f32[1,64,64]{2,1,0:T(8,128)} %param.13) | copy-start | bytes 49156
  3.5 0.8 %copy-start.5 = (f32[1,64,64]{2,1,0:T(8,128)S(1)}, f32[1,64,64]{2,1,0:T(8,128)}, u32[]{:S(2)}) copy-start(f32[1,64,64]{2,1,0:T(8,128)} %param.14) | copy-start | bytes 49156
  44.6 6.2 %collective-permute-start = (bf16[32,32,128]{2,1,0:T(8,128)(2,1)S(1)}, bf16[32,32,128]{2,1,0:T(8,128)(2,1)S(1)}, u32[]{:S(2)}, u32[]{:S(2)}) collective-permute-start(bf16[32,32,128]{2,1,0:T(8,128)(2,1)S(1)} %all_to_all.10), channel_id=1, source_target_pairs={{0,8},{8,0},{1,9},{9,1},{2,10},{10,2},{3,11},{11,3},{4,12},{12,4},... | collective-permute-start | bytes 786440 | tf_op jit(solution)/shard_map/ppermute | solution.py:42
  50.9 1.2 %copy-start.2 = (bf16[1,128,4096]{2,1,0:T(8,128)(2,1)S(1)}, bf16[1,128,4096]{2,1,0:T(8,128)(2,1)}, u32[]{:S(2)}) copy-start(bf16[1,128,4096]{2,1,0:T(8,128)(2,1)} %param.15) | copy-start | bytes 3145732

commit v2 on v1

v2 whole, which is shorter than its diff:
```python
import functools
import jax
import jax.numpy as jnp
from jax import lax
from jax.experimental import pallas as pl
from jax.experimental.pallas import tpu as pltpu
from jax.sharding import Mesh, PartitionSpec as P

PIECES = 4


def _own_kernel(copies, x_hbm, c_hbm, n_ref, pi_hbm, po_hbm, a_hbm, b_hbm, o_ref, x, c, pi, po, a, b, sems):
    length, width = x.shape
    rank = pi.shape[0]
    step = width // PIECES
    started = []
    for p in range(PIECES):
        cols = pl.ds(p * step, step)
        group = [
            pltpu.make_async_copy(src.at[:, cols], dst.at[:, cols], sems.at[4 * p + i])
            for i, (src, dst) in enumerate(((c_hbm, c), (po_hbm, po), (x_hbm, x), (pi_hbm, pi)))
        ]
        for copy in group:
            copy.start()
        started.append(group)
    factors = [
        pltpu.make_async_copy(a_hbm, a, sems.at[4 * PIECES]),
        pltpu.make_async_copy(b_hbm, b, sems.at[4 * PIECES + 1]),
    ]
    for copy in factors:
        copy.start()
    out_side = jnp.zeros((rank, length), jnp.float32)
    in_side = jnp.zeros((length, rank), jnp.float32)
    nt = (((1,), (1,)), ((), ()))
    for p in range(PIECES):
        cols = pl.ds(p * step, step)
        group = started[p]
        group[0].wait()
        group[1].wait()
        out_side += lax.dot_general(po[:, cols], c[:, cols], nt, preferred_element_type=jnp.float32)
        group[2].wait()
        group[3].wait()
        in_side += lax.dot_general(x[:, cols], pi[:, cols], nt, preferred_element_type=jnp.float32)
    slots = lax.broadcasted_iota(jnp.int32, (rank, length), 1)
    out_side = jnp.where(slots < n_ref[0], out_side, 0.0).astype(jnp.bfloat16)
    grad = jnp.dot(out_side, in_side.astype(jnp.bfloat16), preferred_element_type=jnp.float32)
    grad = grad.astype(jnp.bfloat16).astype(jnp.float32)
    for copy in factors:
        copy.wait()
    half = rank // 2
    rows = jnp.concatenate([a[pl.ds(0, half, stride=2), :], a[pl.ds(1, half, stride=2), :]], axis=0)
    left = jnp.dot(rows, grad, precision=lax.Precision.HIGHEST, preferred_element_type=jnp.float32)
    both = jnp.dot(left, b[...], precision=lax.Precision.HIGHEST, preferred_element_type=jnp.float32)
    paired = jnp.concatenate([both[:half], both[half:]], axis=1).astype(jnp.bfloat16)
    for i in range(copies):
        o_ref[i] = paired


def own_gradient(copies, x, c, n, pi, po, a, b):
    length, width = x.shape
    rank = pi.shape[0]
    any_ = pl.BlockSpec(memory_space=pltpu.HBM)
    return pl.pallas_call(
        functools.partial(_own_kernel, copies),
        out_shape=jax.ShapeDtypeStruct((copies, rank // 2, 2 * rank), jnp.bfloat16),
        in_specs=[any_, any_, pl.BlockSpec(memory_space=pltpu.SMEM), any_, any_, any_, any_],
        out_specs=pl.BlockSpec(memory_space=pltpu.VMEM),
        scratch_shapes=[
            pltpu.VMEM((length, width), jnp.bfloat16),
            pltpu.VMEM((length, width), jnp.bfloat16),
            pltpu.VMEM((rank, width), jnp.bfloat16),
            pltpu.VMEM((rank, width), jnp.bfloat16),
            pltpu.VMEM((rank, rank), jnp.float32),
            pltpu.VMEM((rank, rank), jnp.float32),
            pltpu.SemaphoreType.DMA((4 * PIECES + 2,)),
        ],
        compiler_params=pltpu.CompilerParams(vmem_limit_bytes=56 * 1024 * 1024),
        name="own_gradient",
    )(x, c, n, pi, po, a, b)

CORES = 2
Y_HI = 2
Y_LO = 2
Z_FIRST = 8
LAYER_FIRST = 7


def turned(count, first):
    return [[(i + first) % count for i in range(count)]]


def swapped(held, axis):
    other = lax.ppermute(held, axis, [(0, 1), (1, 0)])
    lower = lax.axis_index(axis) == 0
    return jnp.stack([jnp.where(lower, held, other), jnp.where(lower, other, held)])


def body(
    query_inputs,
    query_cotangents,
    query_lengths,
    proj_in,
    proj_out,
    out_factor,
    in_factor,
    train_grads,
):
    flat = train_grads.shape[2]
    train = train_grads.shape[1]
    places = lax.axis_size("z")
    sent = own_gradient(
        places,
        query_inputs[0, 0],
        query_cotangents[0, 0],
        query_lengths,
        proj_in[0],
        proj_out[0],
        out_factor[0],
        in_factor[0],
    )
    held = lax.all_to_all(sent, "z", 0, 0, axis_index_groups=turned(places, Z_FIRST))
    held = swapped(held, "yh")
    held = swapped(held, "core")
    queries = held.reshape(-1, flat)
    partial = lax.dot_general(
        queries, train_grads[0], (((1,), (1,)), ((), ())), preferred_element_type=jnp.float32
    )
    partial = partial.reshape(CORES, Y_HI, places, train)
    partial = jnp.roll(partial, Z_FIRST, axis=2).transpose(1, 2, 0, 3)
    layers = lax.axis_size(("x", "yl"))
    partial = partial.reshape(layers, -1, train)
    partial = jnp.roll(partial, -LAYER_FIRST, axis=0)
    terms = lax.all_to_all(
        partial, ("x", "yl"), 0, 0, axis_index_groups=turned(layers, LAYER_FIRST)
    )
    return jnp.sum(terms, axis=0)


def solution(mesh):
    dp, layer = mesh.devices.shape
    shape = (Y_HI, dp // (Y_HI * CORES), CORES, layer // Y_LO, Y_LO)
    fine = Mesh(mesh.devices.reshape(shape), ("yh", "z", "core", "x", "yl"))
    dp, layer = ("yh", "z", "core"), ("x", "yl")
    in_specs = (
        P(layer, dp, None, None),
        P(layer, dp, None, None),
        P(dp),
        P(layer, None, None),
        P(layer, None, None),
        P(layer, None, None),
        P(layer, None, None),
        P(layer, dp, None),
    )
    return jax.shard_map(
        body, mesh=fine, in_specs=in_specs, out_specs=P(layer, dp), check_vma=False
    )
```

time: 62.6 us -> 53.4 us (0.85)
  blocking collectives: 49 us -> 34 us
  starting transfers between devices: 5.09 us -> 9.15 us
  Pallas kernels: 0 us -> 4.01 us
  matrix products: 3.02 us -> 0.48 us
  waiting for transfers between devices: 1.13 us -> 3.51 us
  local copies, waits for them, and re-layouts: 2.41 us -> 0.27 us
    all_to_all x2, blocking collectives: 49 us -> 34 us  [the longest x1 25.6 us: body(): lax.all_to_all(sent, 'z', 0, 0, axis_index_groups=turned(places, Z_FIRST))]
    ppermute x1 -> x2, starting transfers between devices: 5.09 us -> 9.15 us  [swapped(): other = lax.ppermute(held, axis, [(0, 1), (1, 0)])]
    pallas_call x0 -> x1, Pallas kernels: none -> 4.01 us  [own_gradient(): pl.pallas_call(functools.partial(_own_kernel, copies), out_shape=jax.Shap...]
    dot_general x4 -> x0, matrix products: 2.54 us -> none  [the longest x1 1.52 us: body(): jnp.einsum('ld,rd->lr', query_inputs[0, 0], proj_in[0], preferred_element...]
    ppermute x1 -> x2, waiting for transfers between devices: 1.13 us -> 3.51 us  [swapped(): other = lax.ppermute(held, axis, [(0, 1), (1, 0)])]
    unnamed x12 -> x2, local copies, waits for them, and re-layouts: 2.06 us -> 0.01 us
  transfers between devices with their start and end apart: 1 -> 2, of which waited for: 1 -> 2; matrix products, arithmetic and copies ran while one was open for 0% -> 0% of each run, Pallas kernels for 0% -> 0%
where the time goes in v2:
time: 53.4 us; the launch traced here: 53 us
  blocking collectives  34 us (64%)
  starting transfers between devices  9.15 us (17%)
  Pallas kernels  4.01 us (8%)
  waiting for transfers between devices  3.51 us (7%)
  between operations  0.87 us (2%)
  other arithmetic  0.7 us (1%)
    all_to_all x1, blocking collectives, body(): lax.all_to_all(sent, 'z', 0, 0, axis_index_groups=turned(places, Z_FIRST))  25.6 us
    ppermute x2, starting transfers between devices, swapped(): other = lax.ppermute(held, axis, [(0, 1), (1, 0)])  9.15 us
    all_to_all x1, blocking collectives, body(): lax.all_to_all(partial, ('x', 'yl'), 0, 0, axis_index_groups=turned(layer...  8.42 us
    pallas_call x1, Pallas kernels, own_gradient(): pl.pallas_call(functools.partial(_own_kernel, copies), out_shape=jax.Shap...  4.01 us
    ppermute x2, waiting for transfers between devices, swapped(): other = lax.ppermute(held, axis, [(0, 1), (1, 0)])  3.51 us
  transfers between devices with their start and end apart: 2, of which 2 were waited for; matrix products, arithmetic and copies ran while one was open for 0% of the time, Pallas kernels for 0%

profile of v2, /device:TPU:1, one launch (start us, length us, event | category | flops | bytes accessed | tf_op | source)
XLA Modules:
  0.0 53.0 jit_solution(16682710777265426604)
XLA Ops:
  0.0 0.0 copy-start
  0.7 4.0 %own_gradient.1 = bf16[16,32,128]{2,1,0:T(8,128)(2,1)} custom-call(bf16[128,4096]{1,0:T(8,128)(2,1)} %bitcast.24, bf16[128,4096]{1,0:T(8,128)(2,1)} %bitcast.25, s32[1]{0:T(128)S(6)} %copy.11.n_ref, bf16[64,4096]{1,0:T(8,128)(2,1)} %bitcast.26, bf16[64,4096]{1,0:T(8,128)(2,1)} %bitcast.27, f32[64,64]{1,0:T(8,128)} %bitcast.30, f32[64,64]{1,0:T(8,128)} %bitcast.31), custom_call_target="tpu_custom_call" | custom-call | tf_op jit(solution)/shard_map/own_gradient/pallas_call | solution.py:63
  4.8 25.6 %all_to_all.10 = bf16[16,32,128]{2,1,0:T(8,128)(2,1)S(1)} all-to-all(bf16[16,32,128]{2,1,0:T(8,128)(2,1)} %own_gradient.1), channel_id=1, replica_groups={{128,144,160,176,192,208,224,240,0,16,32,48,64,80,96,112},{129,145,161,..., dimensions={0} | all-to-all | bytes 262144 | tf_op jit(solution)/shard_map/all_to_all | solution.py:121
  30.4 4.8 %collective-permute-start = (bf16[16,32,128]{2,1,0:T(8,128)(2,1)S(1)}, bf16[16,32,128]{2,1,0:T(8,128)(2,1)S(1)}, u32[]{:S(2)}, u32[]{:S(2)}) collective-permute-start(bf16[16,32,128]{2,1,0:T(8,128)(2,1)S(1)} %all_to_all.10), channel_id=1, source_target_pairs={{0,256},{256,0},{1,257},{257,1},{2,258},{258,2},{3,259},{259,3},{4... | collective-permute-start | bytes 393224 | tf_op jit(solution)/shard_map/ppermute | solution.py:93
  35.2 2.4 %collective-permute-done = bf16[16,32,128]{2,1,0:T(8,128)(2,1)S(1)} collective-permute-done((bf16[16,32,128]{2,1,0:T(8,128)(2,1)S(1)}, bf16[16,32,128]{2,1,0:T(8,128)(2,1)S(1)}, u32[]{:S(2)}, u32[]{:S(2)}) %collective-permute-start) | collective-permute-done | bytes 131104 | tf_op jit(solution)/shard_map/ppermute | solution.py:93
  37.6 4.3 %collective-permute-start.1 = (bf16[2,16,32,128]{3,2,1,0:T(8,128)(2,1)S(1)}, bf16[2,16,32,128]{3,2,1,0:T(8,128)(2,1)S(1)}, u32[]{:S(2)}, u32[]{:S(2)}) collective-permute-start(bf16[2,16,32,128]{3,2,1,0:T(8,128)(2,1)S(1)} %pad_maximum_fusion), channel_id=1, source_target_pairs={{0,8},{8,0},{1,9},{9,1},{2,10},{10,2},{3,11},{11,3},{4,12},{12,4},... | collective-permute-start | bytes 786440 | tf_op jit(solution)/shard_map/ppermute | solution.py:93
  42.0 1.1 %collective-permute-done.1 = bf16[2,16,32,128]{3,2,1,0:T(8,128)(2,1)S(1)} collective-permute-done((bf16[2,16,32,128]{3,2,1,0:T(8,128)(2,1)S(1)}, bf16[2,16,32,128]{3,2,1,0:T(8,128)(2,1)S(1)}, u32[]{:S(2)}, u32[]{:S(2)}) %collective-permute-start.1) | collective-permute-done | bytes 262176 | tf_op jit(solution)/shard_map/ppermute | solution.py:93
  43.1 0.1 stack.21
  43.3 0.1 stack.22
  43.4 0.0 copy-done
  43.4 0.5 fusion
  44.0 8.4 %all_to_all.11 = f32[8,8,128]{2,1,0:T(8,128)S(1)} all-to-all(f32[8,8,128]{2,1,0:T(8,128)S(1)} %pad_maximum_fusion.1), channel_id=1, replica_groups={{7,0,1,2,3,4,5,6},{15,8,9,10,11,12,13,14},{23,16,17,18,19,20,21,22},{31..., dimensions={0} | all-to-all | bytes 65536 | tf_op jit(solution)/shard_map/all_to_all | solution.py:133
  52.4 0.6 %reduce_sum.9 = f32[8,128]{1,0:T(8,128)} reduce(f32[8,8,128]{2,1,0:T(8,128)S(1)} %all_to_all.11, f32[]{:T(128)} %constant.13.clone.1), dimensions={0}, to_apply=%region_0.1 | reduce | flops 7168 | bytes 36868 | tf_op jit(solution)/shard_map/reduce_sum | solution.py:136
  (9 shorter events, 0.1 us)
Async XLA Ops:
  0.0 43.4 %copy-start = (bf16[1,128,4096]{2,1,0:T(8,128)(2,1)S(1)}, bf16[1,128,4096]{2,1,0:T(8,128)(2,1)}, u32[]{:S(2)}) copy-start(bf16[1,128,4096]{2,1,0:T(8,128)(2,1)} %param.15) | copy-start | bytes 3145732
  30.4 7.2 %collective-permute-start = (bf16[16,32,128]{2,1,0:T(8,128)(2,1)S(1)}, bf16[16,32,128]{2,1,0:T(8,128)(2,1)S(1)}, u32[]{:S(2)}, u32[]{:S(2)}) collective-permute-start(bf16[16,32,128]{2,1,0:T(8,128)(2,1)S(1)} %all_to_all.10), channel_id=1, source_target_pairs={{0,256},{256,0},{1,257},{257,1},{2,258},{258,2},{3,259},{259,3},{4... | collective-permute-start | bytes 393224 | tf_op jit(solution)/shard_map/ppermute | solution.py:93
  37.6 5.5 %collective-permute-start.1 = (bf16[2,16,32,128]{3,2,1,0:T(8,128)(2,1)S(1)}, bf16[2,16,32,128]{3,2,1,0:T(8,128)(2,1)S(1)}, u32[]{:S(2)}, u32[]{:S(2)}) collective-permute-start(bf16[2,16,32,128]{3,2,1,0:T(8,128)(2,1)S(1)} %pad_maximum_fusion), channel_id=1, source_target_pairs={{0,8},{8,0},{1,9},{9,1},{2,10},{10,2},{3,11},{11,3},{4,12},{12,4},... | collective-permute-start | bytes 786440 | tf_op jit(solution)/shard_map/ppermute | solution.py:93

commit v3 on v2

--- a/solution.py
+++ b/solution.py
@@ -82,7 +82,6 @@
 Y_HI = 2
 Y_LO = 2
 Z_FIRST = 8
-LAYER_FIRST = 7
 
 
 def turned(count, first):
@@ -118,22 +117,28 @@
         out_factor[0],
         in_factor[0],
     )
+    mine = train_grads[0]
+    theirs = lax.ppermute(mine, "core", [(0, 1), (1, 0)])
     held = lax.all_to_all(sent, "z", 0, 0, axis_index_groups=turned(places, Z_FIRST))
-    held = swapped(held, "yh")
-    held = swapped(held, "core")
-    queries = held.reshape(-1, flat)
-    partial = lax.dot_general(
-        queries, train_grads[0], (((1,), (1,)), ((), ())), preferred_element_type=jnp.float32
+    nt = (((1,), (1,)), ((), ()))
+    layers = lax.axis_size(("x", "yl"))
+
+    def scores(rows):
+        part = lax.dot_general(queries, rows, nt, preferred_element_type=jnp.float32)
+        part = part.reshape(-1, places, train)
+        return jnp.roll(part, Z_FIRST, axis=1)
+
+    queries = swapped(held, "yh").reshape(-1, flat)
+    here, there = scores(mine), scores(theirs)
+    lower = lax.axis_index("core") == 0
+    both = jnp.stack([jnp.where(lower, here, there), jnp.where(lower, there, here)])
+    both = both.reshape(CORES * layers, -1, train)
+    both = jnp.roll(both, 1, axis=0)
+    terms = lax.all_to_all(
+        both, ("core", "x", "yl"), 0, 0, axis_index_groups=turned(CORES * layers, CORES * layers - 1)
     )
-    partial = partial.reshape(CORES, Y_HI, places, train)
-    partial = jnp.roll(partial, Z_FIRST, axis=2).transpose(1, 2, 0, 3)
-    layers = lax.axis_size(("x", "yl"))
-    partial = partial.reshape(layers, -1, train)
-    partial = jnp.roll(partial, -LAYER_FIRST, axis=0)
-    terms = lax.all_to_all(
-        partial, ("x", "yl"), 0, 0, axis_index_groups=turned(layers, LAYER_FIRST)
-    )
-    return jnp.sum(terms, axis=0)
+    terms = jnp.roll(terms, -1, axis=0).reshape((CORES, layers) + terms.shape[1:])
+    return jnp.sum(terms, axis=1).transpose(1, 0, 2).reshape(-1, train)
 
 
 def solution(mesh):

time: 53.4 us -> 51.4 us (0.963)
  waiting for transfers between devices: 3.51 us -> 1.57 us
  starting transfers between devices: 9.15 us -> 8.28 us
  blocking collectives: 34 us -> 34.7 us
  other arithmetic: 0.7 us -> 0.07 us
    ppermute x2 -> x1, starting transfers between devices: 9.15 us -> 4.81 us  [swapped(): other = lax.ppermute(held, axis, [(0, 1), (1, 0)])]
    ppermute x2 -> x1, waiting for transfers between devices: 3.51 us -> 0.01 us  [swapped(): other = lax.ppermute(held, axis, [(0, 1), (1, 0)])]
    ppermute x0 -> x1, starting transfers between devices: none -> 3.47 us  [body(): theirs = lax.ppermute(mine, 'core', [(0, 1), (1, 0)])]
    ppermute x0 -> x1, waiting for transfers between devices: none -> 1.57 us  [body(): theirs = lax.ppermute(mine, 'core', [(0, 1), (1, 0)])]
    all_to_all x1, blocking collectives: 8.42 us -> 9.07 us  [body(): lax.all_to_all(both, ('core', 'x', 'yl'), 0, 0, axis_index_groups=turned(...]
    reduce_sum x1, other arithmetic: 0.6 us -> 0.02 us  [body(): return jnp.sum(terms, axis=1).transpose(1, 0, 2).reshape(-1, train)]
    transpose x1, local copies, waits for them, and re-layouts: 0.03 us -> 0.6 us  [body(): return jnp.sum(terms, axis=1).transpose(1, 0, 2).reshape(-1, train)]
  transfers between devices with their start and end apart: 2 -> 2, of which waited for: 2 -> 1; matrix products, arithmetic and copies ran while one was open for 0% -> 1% of each run, Pallas kernels for 0% -> 0%
where the time goes in v3:
time: 51.4 us; the launch traced here: 51.2 us
  blocking collectives  34.7 us (68%)
  starting transfers between devices  8.28 us (16%)
  Pallas kernels  4.11 us (8%)
  waiting for transfers between devices  1.57 us (3%)
  matrix products  0.89 us (2%)
  between operations  0.81 us (2%)
  local copies, waits for them, and re-layouts  0.79 us (2%)
    all_to_all x1, blocking collectives, body(): lax.all_to_all(sent, 'z', 0, 0, axis_index_groups=turned(places, Z_FIRST))  25.6 us
    all_to_all x1, blocking collectives, body(): lax.all_to_all(both, ('core', 'x', 'yl'), 0, 0, axis_index_groups=turned(...  9.07 us
    ppermute x1, starting transfers between devices, swapped(): other = lax.ppermute(held, axis, [(0, 1), (1, 0)])  4.81 us
    pallas_call x1, Pallas kernels, own_gradient(): pl.pallas_call(functools.partial(_own_kernel, copies), out_shape=jax.Shap...  4.11 us
    ppermute x1, starting transfers between devices, body(): theirs = lax.ppermute(mine, 'core', [(0, 1), (1, 0)])  3.47 us
    ppermute x1, waiting for transfers between devices, body(): theirs = lax.ppermute(mine, 'core', [(0, 1), (1, 0)])  1.57 us
  transfers between devices with their start and end apart: 2, of which 1 were waited for; matrix products, arithmetic and copies ran while one was open for 1% of the time, Pallas kernels for 0%

profile of v3, /device:TPU:1, one launch (start us, length us, event | category | flops | bytes accessed | tf_op | source)
XLA Modules:
  0.0 51.2 jit_solution(7221885322830922502)
XLA Ops:
  0.7 0.0 copy-start
  0.7 4.1 %own_gradient.1 = bf16[16,32,128]{2,1,0:T(8,128)(2,1)} custom-call(bf16[128,4096]{1,0:T(8,128)(2,1)} %bitcast.28, bf16[128,4096]{1,0:T(8,128)(2,1)} %bitcast.29, s32[1]{0:T(128)S(6)} %copy.11.n_ref, bf16[64,4096]{1,0:T(8,128)(2,1)} %bitcast.31, bf16[64,4096]{1,0:T(8,128)(2,1)} %bitcast.32, f32[64,64]{1,0:T(8,128)} %bitcast.35, f32[64,64]{1,0:T(8,128)} %bitcast.36), custom_call_target="tpu_custom_call" | custom-call | tf_op jit(solution)/shard_map/own_gradient/pallas_call | solution.py:63
  4.8 25.6 %all_to_all.10 = bf16[16,32,128]{2,1,0:T(8,128)(2,1)S(1)} all-to-all(bf16[16,32,128]{2,1,0:T(8,128)(2,1)} %own_gradient.1), channel_id=1, replica_groups={{128,144,160,176,192,208,224,240,0,16,32,48,64,80,96,112},{129,145,161,..., dimensions={0} | all-to-all | bytes 262144 | tf_op jit(solution)/shard_map/all_to_all | solution.py:122
  30.4 4.8 %collective-permute-start = (bf16[16,32,128]{2,1,0:T(8,128)(2,1)S(1)}, bf16[16,32,128]{2,1,0:T(8,128)(2,1)S(1)}, u32[]{:S(2)}, u32[]{:S(2)}) collective-permute-start(bf16[16,32,128]{2,1,0:T(8,128)(2,1)S(1)} %all_to_all.10), channel_id=1, source_target_pairs={{0,256},{256,0},{1,257},{257,1},{2,258},{258,2},{3,259},{259,3},{4... | collective-permute-start | bytes 393224 | tf_op jit(solution)/shard_map/ppermute | solution.py:92
  35.2 0.0 copy-done
  35.2 3.5 %collective-permute-start.1 = (bf16[128,4096]{1,0:T(8,128)(2,1)S(1)}, bf16[128,4096]{1,0:T(8,128)(2,1)S(1)}, u32[]{:S(2)}, u32[]{:S(2)}) collective-permute-start(bf16[128,4096]{1,0:T(8,128)(2,1)S(1)} %bitcast.30), channel_id=1, source_target_pairs={{0,8},{8,0},{1,9},{9,1},{2,10},{10,2},{3,11},{11,3},{4,12},{12,4},... | collective-permute-start | bytes 3145736 | tf_op jit(solution)/shard_map/ppermute | solution.py:121
  38.7 0.0 collective-permute-done
  38.7 0.1 stack.14
  38.8 0.1 stack.15
  38.9 0.4 fusion.2
  39.4 1.6 %collective-permute-done.1 = bf16[128,4096]{1,0:T(8,128)(2,1)S(1)} collective-permute-done((bf16[128,4096]{1,0:T(8,128)(2,1)S(1)}, bf16[128,4096]{1,0:T(8,128)(2,1)S(1)}, u32[]{:S(2)}, u32[]{:S(2)}) %collective-permute-start.1) | collective-permute-done | bytes 1048608 | tf_op jit(solution)/shard_map/ppermute | solution.py:121
  40.9 0.4 fusion
  41.5 9.1 %all_to_all.11 = f32[16,4,128]{2,1,0:T(4,128)S(1)} all-to-all(f32[16,4,128]{2,1,0:T(4,128)S(1)} %pad_maximum_fusion.1), channel_id=1, replica_groups={{15,0,1,2,3,4,5,6,7,8,9,10,11,12,13,14},{31,16,17,18,19,20,21,22,23,24,..., dimensions={0} | all-to-all | bytes 65536 | tf_op jit(solution)/shard_map/all_to_all | solution.py:137
  50.6 0.6 %copy.9 = f32[4,2,128]{2,1,0:T(2,128)} copy(f32[4,2,128]{2,0,1:T(4,128)S(1)} %bitcast.37) | data formatting | bytes 8192 | tf_op jit(solution)/shard_map/transpose | solution.py:141
  (13 shorter events, 0.1 us)
Async XLA Ops:
  0.7 34.5 %copy-start = (bf16[1,128,4096]{2,1,0:T(8,128)(2,1)S(1)}, bf16[1,128,4096]{2,1,0:T(8,128)(2,1)}, u32[]{:S(2)}) copy-start(bf16[1,128,4096]{2,1,0:T(8,128)(2,1)} %param.15) | copy-start | bytes 3145732
  30.4 8.3 %collective-permute-start = (bf16[16,32,128]{2,1,0:T(8,128)(2,1)S(1)}, bf16[16,32,128]{2,1,0:T(8,128)(2,1)S(1)}, u32[]{:S(2)}, u32[]{:S(2)}) collective-permute-start(bf16[16,32,128]{2,1,0:T(8,128)(2,1)S(1)} %all_to_all.10), channel_id=1, source_target_pairs={{0,256},{256,0},{1,257},{257,1},{2,258},{258,2},{3,259},{259,3},{4... | collective-permute-start | bytes 393224 | tf_op jit(solution)/shard_map/ppermute | solution.py:92
  35.2 5.7 %collective-permute-start.1 = (bf16[128,4096]{1,0:T(8,128)(2,1)S(1)}, bf16[128,4096]{1,0:T(8,128)(2,1)S(1)}, u32[]{:S(2)}, u32[]{:S(2)}) collective-permute-start(bf16[128,4096]{1,0:T(8,128)(2,1)S(1)} %bitcast.30), channel_id=1, source_target_pairs={{0,8},{8,0},{1,9},{9,1},{2,10},{10,2},{3,11},{11,3},{4,12},{12,4},... | collective-permute-start | bytes 3145736 | tf_op jit(solution)/shard_map/ppermute | solution.py:121

commit v4 on v2

v4 whole, which is shorter than its diff:
```python
import functools
import jax
import jax.numpy as jnp
from jax import lax
from jax.experimental import pallas as pl
from jax.experimental.pallas import tpu as pltpu
from jax.sharding import Mesh, PartitionSpec as P

PIECES = 4


def _own_kernel(copies, x_hbm, c_hbm, n_hbm, pi_hbm, po_hbm, a_hbm, b_hbm, o_ref, x, c, n, pi, po, a, b, sems):
    length, width = x.shape
    rank = pi.shape[0]
    step = width // PIECES
    started = []
    for p in range(PIECES):
        cols = pl.ds(p * step, step)
        group = [
            pltpu.make_async_copy(src.at[:, cols], dst.at[:, cols], sems.at[4 * p + i])
            for i, (src, dst) in enumerate(((c_hbm, c), (po_hbm, po), (x_hbm, x), (pi_hbm, pi)))
        ]
        for copy in group:
            copy.start()
        started.append(group)
    factors = [
        pltpu.make_async_copy(a_hbm, a, sems.at[4 * PIECES]),
        pltpu.make_async_copy(b_hbm, b, sems.at[4 * PIECES + 1]),
        pltpu.make_async_copy(n_hbm, n, sems.at[4 * PIECES + 2]),
    ]
    for copy in factors:
        copy.start()
    out_side = jnp.zeros((rank, length), jnp.float32)
    in_side = jnp.zeros((length, rank), jnp.float32)
    nt = (((1,), (1,)), ((), ()))
    for p in range(PIECES):
        cols = pl.ds(p * step, step)
        group = started[p]
        group[0].wait()
        group[1].wait()
        out_side += lax.dot_general(po[:, cols], c[:, cols], nt, preferred_element_type=jnp.float32)
        group[2].wait()
        group[3].wait()
        in_side += lax.dot_general(x[:, cols], pi[:, cols], nt, preferred_element_type=jnp.float32)
    for copy in factors:
        copy.wait()
    slots = lax.broadcasted_iota(jnp.int32, (rank, length), 1)
    out_side = jnp.where(slots < n[0], out_side, 0.0).astype(jnp.bfloat16)
    grad = jnp.dot(out_side, in_side.astype(jnp.bfloat16), preferred_element_type=jnp.float32)
    grad = grad.astype(jnp.bfloat16).astype(jnp.float32)
    half = rank // 2
    rows = jnp.concatenate([a[pl.ds(0, half, stride=2), :], a[pl.ds(1, half, stride=2), :]], axis=0)
    left = jnp.dot(rows, grad, precision=lax.Precision.HIGHEST, preferred_element_type=jnp.float32)
    both = jnp.dot(left, b[...], precision=lax.Precision.HIGHEST, preferred_element_type=jnp.float32)
    paired = jnp.concatenate([both[:half], both[half:]], axis=1).astype(jnp.bfloat16)
    for i in range(copies):
        o_ref[i] = paired


def own_gradient(copies, x, c, n, pi, po, a, b):
    length, width = x.shape
    rank = pi.shape[0]
    any_ = pl.BlockSpec(memory_space=pl.ANY)
    return pl.pallas_call(
        functools.partial(_own_kernel, copies),
        out_shape=jax.ShapeDtypeStruct((copies, rank // 2, 2 * rank), jnp.bfloat16),
        in_specs=[any_, any_, pl.BlockSpec(memory_space=pltpu.HBM)] + [any_] * 4,
        out_specs=pl.BlockSpec(memory_space=pltpu.VMEM),
        scratch_shapes=[
            pltpu.VMEM((length, width), jnp.bfloat16),
            pltpu.VMEM((length, width), jnp.bfloat16),
            pltpu.SMEM((1,), jnp.int32),
            pltpu.VMEM((rank, width), jnp.bfloat16),
            pltpu.VMEM((rank, width), jnp.bfloat16),
            pltpu.VMEM((rank, rank), jnp.float32),
            pltpu.VMEM((rank, rank), jnp.float32),
            pltpu.SemaphoreType.DMA((4 * PIECES + 3,)),
        ],
        compiler_params=pltpu.CompilerParams(vmem_limit_bytes=16 * 1024 * 1024),
        name="own_gradient",
    )(x, c, n, pi, po, a, b)


CORES = 2
Y_HI = 2
Y_LO = 2
RUN = 4


def runs_of(places):
    half = places // RUN // 2
    return [r for i in range(half) for r in (half + i, i)]


def swap(array, axis):
    return lax.ppermute(array, axis, [(0, 1), (1, 0)])


def last_first(count):
    return [[(i + count - 1) % count for i in range(count)]]


def own_sent(query_inputs, query_cotangents, query_lengths, proj_in, proj_out, out_factor, in_factor):
    return own_gradient(
        lax.axis_size("z"),
        pltpu.with_memory_space_constraint(query_inputs[0, 0], pltpu.HBM),
        pltpu.with_memory_space_constraint(query_cotangents[0, 0], pltpu.HBM),
        query_lengths,
        pltpu.with_memory_space_constraint(proj_in[0], pltpu.HBM),
        pltpu.with_memory_space_constraint(proj_out[0], pltpu.HBM),
        pltpu.with_memory_space_constraint(out_factor[0], pltpu.HBM),
        pltpu.with_memory_space_constraint(in_factor[0], pltpu.HBM),
    )


def gathered(sent):
    places = lax.axis_size("z")
    order = [r * RUN + i for r in runs_of(places) for i in range(RUN)]
    return lax.all_to_all(sent, "z", 0, 0, axis_index_groups=[order])


def both_scores(q_ref, more_ref, mine_ref, theirs_ref):
    nt = (((1,), (1,)), ((), ()))
    q = jnp.concatenate([q_ref[...], more_ref[...]], axis=0)
    mine = lax.dot_general(q, mine_ref[...], nt, preferred_element_type=jnp.float32)
    theirs = lax.dot_general(q, theirs_ref[...], nt, preferred_element_type=jnp.float32)
    return mine, theirs


def scored(kernel, shape, queries, more, mine, theirs):
    vmem = pl.BlockSpec(memory_space=pltpu.VMEM)
    return pl.pallas_call(
        kernel,
        out_shape=jax.ShapeDtypeStruct(shape, jnp.float32),
        in_specs=[vmem] * 4,
        out_specs=vmem,
        compiler_params=pltpu.CompilerParams(vmem_limit_bytes=16 * 1024 * 1024),
        name="scored",
    )(queries, more, mine, theirs)


def _score_kernel(places, q_ref, more_ref, mine_ref, theirs_ref, o_ref):
    mine, theirs = both_scores(q_ref, more_ref, mine_ref, theirs_ref)
    core, yh = lax.axis_index("core"), lax.axis_index("yh")
    blocks = o_ref.shape[0]
    runs = runs_of(places)
    for h in range(Y_HI):
        part = jnp.where(yh == h, mine, theirs)
        first = jnp.where(core == 0, part[:places], part[places:])
        second = jnp.where(core == 0, part[places:], part[:places])
        for i, r in enumerate(runs):
            rows = slice(i * RUN, (i + 1) * RUN)
            block = jnp.concatenate([first[rows], second[rows]], axis=0)
            for half in range(Y_HI):
                o_ref[((h * Y_HI + half) * len(runs) + r + 1) % blocks] = block


def body(
    query_inputs,
    query_cotangents,
    query_lengths,
    proj_in,
    proj_out,
    out_factor,
    in_factor,
    train_grads,
):
    flat = train_grads.shape[2]
    train = train_grads.shape[1]
    places = lax.axis_size("z")
    layers = lax.axis_size(("x", "yl"))
    mine = train_grads[0]
    sent = own_sent(
        query_inputs, query_cotangents, query_lengths, proj_in, proj_out, out_factor, in_factor
    )
    ahead = mine
    theirs = swap(ahead, "yh")
    held = gathered(sent)
    held, theirs = lax.optimization_barrier((held, theirs))
    more = swap(held, "core")
    parts = scored(
        functools.partial(_score_kernel, places),
        (Y_HI * layers, CORES * RUN, train),
        held.reshape(places, flat),
        more.reshape(places, flat),
        mine,
        theirs,
    )
    asked = lax.axis_index(("x", "yl")) // (layers // Y_HI) == 0
    parts, asked = lax.optimization_barrier((parts, asked))
    terms = lax.all_to_all(
        parts, ("yh", "x", "yl"), 0, 0, axis_index_groups=last_first(Y_HI * layers)
    )
    terms = jnp.roll(terms, -1, axis=0).reshape((Y_HI, layers) + terms.shape[1:])
    terms = jnp.sum(jnp.where(asked, terms[0], terms[1]), axis=0)
    return terms.reshape(CORES, RUN, train).transpose(1, 0, 2).reshape(-1, train)


def solution(mesh):
    dp, layer = mesh.devices.shape
    shape = (Y_HI, dp // (Y_HI * CORES), CORES, layer // Y_LO, Y_LO)
    fine = Mesh(mesh.devices.reshape(shape), ("yh", "z", "core", "x", "yl"))
    dp, layer = ("yh", "z", "core"), ("x", "yl")
    in_specs = (
        P(layer, dp, None, None),
        P(layer, dp, None, None),
        P(dp),
        P(layer, None, None),
        P(layer, None, None),
        P(layer, None, None),
        P(layer, None, None),
        P(layer, dp, None),
    )
    return jax.shard_map(
        body, mesh=fine, in_specs=in_specs, out_specs=P(layer, dp), check_vma=False
    )
```

time: 53.4 us -> 50.2 us (0.940)
  waiting for transfers between devices: 3.51 us -> 0.89 us
  starting transfers between devices: 9.15 us -> 10 us
  blocking collectives: 34 us -> 33.3 us
  other arithmetic: 0.7 us -> 0.01 us
    ppermute x2, waiting for transfers between devices: 3.51 us -> 0.89 us  [swap(): return lax.ppermute(array, axis, [(0, 1), (1, 0)])]
    ppermute x2, starting transfers between devices: 9.15 us -> 10 us  [swap(): return lax.ppermute(array, axis, [(0, 1), (1, 0)])]
    pallas_call x0 -> x1, Pallas kernels: none -> 0.81 us  [scored(): pl.pallas_call(kernel, out_shape=jax.ShapeDtypeStruct(shape, jnp.float32)...]
    all_to_all x2, blocking collectives: 34 us -> 33.3 us  [the longest x1 23.1 us: gathered(): return lax.all_to_all(sent, 'z', 0, 0, axis_index_groups=[order])]
    reduce_sum x1, other arithmetic: 0.6 us -> 0.01 us  [body(): terms = jnp.sum(jnp.where(asked, terms[0], terms[1]), axis=0)]
    transpose x1, local copies, waits for them, and re-layouts: 0.03 us -> 0.6 us  [body(): terms.reshape(CORES, RUN, train).transpose(1, 0, 2).reshape(-1, train)]
  transfers between devices with their start and end apart: 2 -> 2, of which waited for: 2 -> 1; matrix products, arithmetic and copies ran while one was open for 0% -> 0% of each run, Pallas kernels for 0% -> 7%
where the time goes in v4:
time: 50.2 us; the launch traced here: 49.9 us
  blocking collectives  33.3 us (66%)
  starting transfers between devices  10 us (20%)
  Pallas kernels  4.3 us (9%)
  waiting for transfers between devices  0.89 us (2%)
  between operations  0.73 us (1%)
  local copies, waits for them, and re-layouts  0.72 us (1%)
    all_to_all x1, blocking collectives, gathered(): return lax.all_to_all(sent, 'z', 0, 0, axis_index_groups=[order])  23.1 us
    all_to_all x1, blocking collectives, body(): lax.all_to_all(parts, ('yh', 'x', 'yl'), 0, 0, axis_index_groups=last_fir...  10.2 us
    ppermute x2, starting transfers between devices, swap(): return lax.ppermute(array, axis, [(0, 1), (1, 0)])  10 us
    pallas_call x1, Pallas kernels, own_gradient(): pl.pallas_call(functools.partial(_own_kernel, copies), out_shape=jax.Shap...  3.49 us
  transfers between devices with their start and end apart: 2, of which 1 were waited for; matrix products, arithmetic and copies ran while one was open for 0% of the time, Pallas kernels for 7%

profile of v4, /device:TPU:1, one launch (start us, length us, event | category | flops | bytes accessed | tf_op | source)
XLA Modules:
  0.0 49.9 jit_solution(3057442210817841413)
XLA Ops:
  0.0 5.6 %collective-permute-start = (bf16[128,4096]{1,0:T(8,128)(2,1)}, bf16[128,4096]{1,0:T(8,128)(2,1)S(1)}, u32[]{:S(2)}, u32[]{:S(2)}) collective-permute-start(bf16[128,4096]{1,0:T(8,128)(2,1)} %bitcast.19), channel_id=1, source_target_pairs={{0,256},{256,0},{1,257},{257,1},{2,258},{258,2},{3,259},{259,3},{4... | collective-permute-start | bytes 3145736 | tf_op jit(solution)/shard_map/ppermute | solution.py:96
  6.3 0.0 copy-start
  6.3 3.5 %own_gradient.1 = bf16[16,32,128]{2,1,0:T(8,128)(2,1)S(1)} custom-call(bf16[128,4096]{1,0:T(8,128)(2,1)} %bitcast.23, bf16[128,4096]{1,0:T(8,128)(2,1)} %bitcast.24, s32[1]{0:T(128)S(6)} %copy.16.n_hbm, bf16[64,4096]{1,0:T(8,128)(2,1)} %bitcast.26, bf16[64,4096]{1,0:T(8,128)(2,1)} %bitcast.27, f32[64,64]{1,0:T(8,128)} %bitcast.29, f32[64,64]{1,0:T(8,128)} %bitcast.30), custom_call_target="tpu_custom_call" | custom-call | tf_op jit(solution)/shard_map/own_gradient/pallas_call | solution.py:64
  9.8 23.1 %all_to_all.10 = bf16[16,32,128]{2,1,0:T(8,128)(2,1)S(1)} all-to-all(bf16[16,32,128]{2,1,0:T(8,128)(2,1)S(1)} %own_gradient.1), channel_id=1, replica_groups={{128,144,160,176,0,16,32,48,192,208,224,240,64,80,96,112},{129,145,161,..., dimensions={0} | all-to-all | bytes 262144 | tf_op jit(solution)/shard_map/all_to_all | solution.py:119
  32.9 0.0 collective-permute-done.theirs_ref
  32.9 4.4 %collective-permute-start.1 = (bf16[16,32,128]{2,1,0:T(8,128)(2,1)S(1)}, bf16[16,32,128]{2,1,0:T(8,128)(2,1)S(1)}, u32[]{:S(2)}, u32[]{:S(2)}) collective-permute-start(bf16[16,32,128]{2,1,0:T(8,128)(2,1)S(1)} %all_to_all.10), channel_id=1, source_target_pairs={{0,8},{8,0},{1,9},{9,1},{2,10},{10,2},{3,11},{11,3},{4,12},{12,4},... | collective-permute-start | bytes 393224 | tf_op jit(solution)/shard_map/ppermute | solution.py:96
  37.3 0.1 copy.15
  37.4 0.9 %collective-permute-done.1 = bf16[16,32,128]{2,1,0:T(8,128)(2,1)S(1)} collective-permute-done((bf16[16,32,128]{2,1,0:T(8,128)(2,1)S(1)}, bf16[16,32,128]{2,1,0:T(8,128)(2,1)S(1)}, u32[]{:S(2)}, u32[]{:S(2)}) %collective-permute-start.1) | collective-permute-done | bytes 131104 | tf_op jit(solution)/shard_map/ppermute | solution.py:96
  38.2 0.1 copy.14
  38.3 0.0 copy-done
  38.3 0.8 %scored.1 = f32[16,8,128]{2,1,0:T(8,128)S(1)} custom-call(bf16[16,4096]{1,0:T(8,128)(2,1)S(1)} %bitcast.21, bf16[16,4096]{1,0:T(8,128)(2,1)S(1)} %bitcast.22, bf16[128,4096]{1,0:T(8,128)(2,1)S(1)} %bitcast.20, bf16[128,4096]{1,0:T(8,128)(2,1)S(1)} %collective-permute-done.theirs_ref), custom_call_target="tpu_custom_call" | custom-call | tf_op jit(solution)/shard_map/scored/pallas_call | solution.py:132
  39.1 10.2 %all_to_all.11 = f32[16,8,128]{2,1,0:T(8,128)S(1)} all-to-all(f32[16,8,128]{2,1,0:T(8,128)S(1)} %scored.1), channel_id=1, replica_groups={{263,0,1,2,3,4,5,6,7,256,257,258,259,260,261,262},{271,8,9,10,11,12,13,..., dimensions={0} | all-to-all | bytes 131072 | tf_op jit(solution)/shard_map/all_to_all | solution.py:191
  49.4 0.6 %copy.9 = f32[4,2,128]{2,1,0:T(2,128)} copy(f32[4,2,128]{2,0,1:T(4,128)S(1)} %bitcast.31) | data formatting | bytes 8192 | tf_op jit(solution)/shard_map/transpose | solution.py:196
  (3 shorter events, 0.0 us)
Async XLA Ops:
  0.0 32.9 %collective-permute-start = (bf16[128,4096]{1,0:T(8,128)(2,1)}, bf16[128,4096]{1,0:T(8,128)(2,1)S(1)}, u32[]{:S(2)}, u32[]{:S(2)}) collective-permute-start(bf16[128,4096]{1,0:T(8,128)(2,1)} %bitcast.19), channel_id=1, source_target_pairs={{0,256},{256,0},{1,257},{257,1},{2,258},{258,2},{3,259},{259,3},{4... | collective-permute-start | bytes 3145736 | tf_op jit(solution)/shard_map/ppermute | solution.py:96
  6.3 32.0 %copy-start = (bf16[1,128,4096]{2,1,0:T(8,128)(2,1)S(1)}, bf16[1,128,4096]{2,1,0:T(8,128)(2,1)}, u32[]{:S(2)}) copy-start(bf16[1,128,4096]{2,1,0:T(8,128)(2,1)} %param.15) | copy-start | bytes 3145732
  32.9 5.4 %collective-permute-start.1 = (bf16[16,32,128]{2,1,0:T(8,128)(2,1)S(1)}, bf16[16,32,128]{2,1,0:T(8,128)(2,1)S(1)}, u32[]{:S(2)}, u32[]{:S(2)}) collective-permute-start(bf16[16,32,128]{2,1,0:T(8,128)(2,1)S(1)} %all_to_all.10), channel_id=1, source_target_pairs={{0,8},{8,0},{1,9},{9,1},{2,10},{10,2},{3,11},{11,3},{4,12},{12,4},... | collective-permute-start | bytes 393224 | tf_op jit(solution)/shard_map/ppermute | solution.py:96

commit v5 on v4

--- a/solution.py
+++ b/solution.py
@@ -85,6 +85,7 @@
 Y_HI = 2
 Y_LO = 2
 RUN = 4
+EARLY = 7
 
 
 def runs_of(places):
@@ -92,8 +93,10 @@
     return [r for i in range(half) for r in (half + i, i)]
 
 
-def swap(array, axis):
-    return lax.ppermute(array, axis, [(0, 1), (1, 0)])
+def pairs(planes, places):
+    over_y = [(h * places + z, (1 - h) * places + z) for z in planes for h in range(Y_HI)]
+    over_core = [(CORES * z + c, CORES * z + 1 - c) for z in planes for c in range(CORES)]
+    return over_y, over_core
 
 
 def last_first(count):
@@ -119,40 +122,87 @@
     return lax.all_to_all(sent, "z", 0, 0, axis_index_groups=[order])
 
 
-def both_scores(q_ref, more_ref, mine_ref, theirs_ref):
+def _mine_kernel(q_ref, core_q_ref, yh_q_ref, mine_ref, o_ref):
     nt = (((1,), (1,)), ((), ()))
-    q = jnp.concatenate([q_ref[...], more_ref[...]], axis=0)
-    mine = lax.dot_general(q, mine_ref[...], nt, preferred_element_type=jnp.float32)
-    theirs = lax.dot_general(q, theirs_ref[...], nt, preferred_element_type=jnp.float32)
-    return mine, theirs
-
-
-def scored(kernel, shape, queries, more, mine, theirs):
+    z = lax.axis_index("z")
+
+    def score(more_ref):
+        q = jnp.concatenate([q_ref[...], more_ref[...]], axis=0)
+        o_ref[...] = lax.dot_general(q, mine_ref[...], nt, preferred_element_type=jnp.float32)
+
+    @pl.when(z < EARLY)
+    def _():
+        score(core_q_ref)
+
+    @pl.when(z >= EARLY)
+    def _():
+        score(yh_q_ref)
+
+
+def scored_mine(*operands):
     vmem = pl.BlockSpec(memory_space=pltpu.VMEM)
+    rows, train = 2 * operands[0].shape[0], operands[3].shape[0]
     return pl.pallas_call(
-        kernel,
-        out_shape=jax.ShapeDtypeStruct(shape, jnp.float32),
+        _mine_kernel,
+        out_shape=jax.ShapeDtypeStruct((rows, train), jnp.float32),
         in_specs=[vmem] * 4,
         out_specs=vmem,
         compiler_params=pltpu.CompilerParams(vmem_limit_bytes=16 * 1024 * 1024),
+        cost_estimate=pl.CostEstimate(flops=10000000000, bytes_accessed=1 << 20, transcendentals=0),
+        name="scored_mine",
+    )(*operands)
+
+
+def _score_kernel(places, q_ref, core_q_ref, yh_q_ref, mine_s, yh_ref, core_ref, o_ref, other_s):
+    nt = (((1,), (1,)), ((), ()))
+    yh, core, z = lax.axis_index("yh"), lax.axis_index("core"), lax.axis_index("z")
+    blocks = o_ref.shape[0]
+    layers = blocks // (Y_HI * CORES)
+    runs = runs_of(places)
+    o_ref[...] = jnp.zeros(o_ref.shape, o_ref.dtype)
+
+    def score(more_ref, other_ref):
+        q = jnp.concatenate([q_ref[...], more_ref[...]], axis=0)
+        other_s[...] = lax.dot_general(q, other_ref[...], nt, preferred_element_type=jnp.float32)
+
+    def put(h, c, layer, first, second):
+        rows = jnp.concatenate([first, second], axis=0)
+        o_ref[lax.rem((h * CORES + c) * layers + layer + 1, blocks)] = rows
+
+    @pl.when(z < EARLY)
+    def _():
+        score(core_q_ref, yh_ref)
+        for s, h in ((mine_s, yh), (other_s, 1 - yh)):
+            for i, r in enumerate(runs):
+                own = s[i * RUN : (i + 1) * RUN]
+                more = s[places + i * RUN : places + (i + 1) * RUN]
+                first = jnp.where(core == 0, own, more)
+                put(h, core, yh * len(runs) + r, first, jnp.where(core == 0, more, own))
+
+    @pl.when(z >= EARLY)
+    def _():
+        score(yh_q_ref, core_ref)
+        for s, c in ((mine_s, core), (other_s, 1 - core)):
+            for half, h in ((0, yh), (1, 1 - yh)):
+                for i, r in enumerate(runs):
+                    at = half * places + i * RUN
+                    own = s[at : at + RUN]
+                    none = jnp.zeros_like(own)
+                    put(yh, c, h * len(runs) + r, jnp.where(core == 0, own, none), jnp.where(core == 0, none, own))
+
+
+def scored(places, layers, *operands):
+    train = operands[3].shape[1]
+    vmem = pl.BlockSpec(memory_space=pltpu.VMEM)
+    return pl.pallas_call(
+        functools.partial(_score_kernel, places),
+        out_shape=jax.ShapeDtypeStruct((Y_HI * CORES * layers, CORES * RUN, train), jnp.float32),
+        in_specs=[vmem] * 6,
+        out_specs=vmem,
+        scratch_shapes=[pltpu.VMEM((2 * places, train), jnp.float32)],
+        compiler_params=pltpu.CompilerParams(vmem_limit_bytes=16 * 1024 * 1024),
         name="scored",
-    )(queries, more, mine, theirs)
-
-
-def _score_kernel(places, q_ref, more_ref, mine_ref, theirs_ref, o_ref):
-    mine, theirs = both_scores(q_ref, more_ref, mine_ref, theirs_ref)
-    core, yh = lax.axis_index("core"), lax.axis_index("yh")
-    blocks = o_ref.shape[0]
-    runs = runs_of(places)
-    for h in range(Y_HI):
-        part = jnp.where(yh == h, mine, theirs)
-        first = jnp.where(core == 0, part[:places], part[places:])
-        second = jnp.where(core == 0, part[places:], part[:places])
-        for i, r in enumerate(runs):
-            rows = slice(i * RUN, (i + 1) * RUN)
-            block = jnp.concatenate([first[rows], second[rows]], axis=0)
-            for half in range(Y_HI):
-                o_ref[((h * Y_HI + half) * len(runs) + r + 1) % blocks] = block
+    )(*operands)
 
 
 def body(
@@ -170,29 +220,22 @@
     places = lax.axis_size("z")
     layers = lax.axis_size(("x", "yl"))
     mine = train_grads[0]
+    early_yh, early_core = pairs(range(EARLY), places)
+    late_yh, late_core = pairs(range(EARLY, places), places)
     sent = own_sent(
         query_inputs, query_cotangents, query_lengths, proj_in, proj_out, out_factor, in_factor
     )
-    ahead = mine
-    theirs = swap(ahead, "yh")
-    held = gathered(sent)
-    held, theirs = lax.optimization_barrier((held, theirs))
-    more = swap(held, "core")
-    parts = scored(
-        functools.partial(_score_kernel, places),
-        (Y_HI * layers, CORES * RUN, train),
-        held.reshape(places, flat),
-        more.reshape(places, flat),
-        mine,
-        theirs,
-    )
-    asked = lax.axis_index(("x", "yl")) // (layers // Y_HI) == 0
-    parts, asked = lax.optimization_barrier((parts, asked))
+    yh_rows = lax.ppermute(mine, ("yh", "z"), early_yh)
+    held, yh_rows, after = lax.optimization_barrier((gathered(sent), yh_rows, mine))
+    yh_queries = lax.ppermute(held, ("yh", "z"), late_yh)
+    core_queries = lax.ppermute(held, ("z", "core"), early_core)
+    core_rows = lax.ppermute(after, ("z", "core"), late_core)
+    queries = [q.reshape(places, flat) for q in (held, core_queries, yh_queries)]
+    parts = scored(places, layers, *queries, scored_mine(*queries, mine), yh_rows, core_rows)
     terms = lax.all_to_all(
-        parts, ("yh", "x", "yl"), 0, 0, axis_index_groups=last_first(Y_HI * layers)
-    )
-    terms = jnp.roll(terms, -1, axis=0).reshape((Y_HI, layers) + terms.shape[1:])
-    terms = jnp.sum(jnp.where(asked, terms[0], terms[1]), axis=0)
+        parts, ("yh", "core", "x", "yl"), 0, 0, axis_index_groups=last_first(parts.shape[0])
+    )
+    terms = jnp.sum(terms, axis=0)
     return terms.reshape(CORES, RUN, train).transpose(1, 0, 2).reshape(-1, train)
 
 

time: 50.2 us -> 49.7 us (0.990)
  blocking collectives: 33.3 us -> 31.7 us
  starting transfers between devices: 10 us -> 11.4 us
  waiting for transfers between devices: 0.89 us -> 0.11 us
    all_to_all x1, blocking collectives: 23.1 us -> 19 us  [gathered(): return lax.all_to_all(sent, 'z', 0, 0, axis_index_groups=[order])]
    all_to_all x1, blocking collectives: 10.2 us -> 12.7 us  [body(): lax.all_to_all(parts, ('yh', 'core', 'x', 'yl'), 0, 0, axis_index_groups=...]
    ppermute x2 -> x4, starting transfers between devices: 10 us -> 11.4 us  [the longest x1 5.64 us: body(): yh_rows = lax.ppermute(mine, ('yh', 'z'), early_yh)]
    ppermute x2 -> x4, waiting for transfers between devices: 0.89 us -> 0.11 us  [the longest x1 0.08 us: body(): core_queries = lax.ppermute(held, ('z', 'core'), early_core)]
  transfers between devices with their start and end apart: 2 -> 4, of which waited for: 1 -> 1; matrix products, arithmetic and copies ran while one was open for 0% -> 0% of each run, Pallas kernels for 7% -> 8%
where the time goes in v5:
time: 49.7 us; the launch traced here: 49.2 us
  blocking collectives  31.7 us (64%)
  starting transfers between devices  11.4 us (23%)
  Pallas kernels  4.42 us (9%)
  local copies, waits for them, and re-layouts  0.77 us (2%)
  between operations  0.74 us (1%)
    all_to_all x1, blocking collectives, gathered(): return lax.all_to_all(sent, 'z', 0, 0, axis_index_groups=[order])  19 us
    all_to_all x1, blocking collectives, body(): lax.all_to_all(parts, ('yh', 'core', 'x', 'yl'), 0, 0, axis_index_groups=...  12.7 us
    ppermute x1, starting transfers between devices, body(): yh_rows = lax.ppermute(mine, ('yh', 'z'), early_yh)  5.64 us
    ppermute x1, starting transfers between devices, body(): core_queries = lax.ppermute(held, ('z', 'core'), early_core)  4.4 us
    pallas_call x1, Pallas kernels, own_gradient(): pl.pallas_call(functools.partial(_own_kernel, copies), out_shape=jax.Shap...  3.49 us
  transfers between devices with their start and end apart: 4, of which 1 were waited for; matrix products, arithmetic and copies ran while one was open for 0% of the time, Pallas kernels for 8%

profile of v5, /device:TPU:1, one launch (start us, length us, event | category | flops | bytes accessed | tf_op | source)
XLA Modules:
  0.0 49.2 jit_solution(4346467030856346804)
XLA Ops:
  0.0 5.6 %collective-permute-start = (bf16[128,4096]{1,0:T(8,128)(2,1)}, bf16[128,4096]{1,0:T(8,128)(2,1)S(1)}, u32[]{:S(2)}, u32[]{:S(2)}) collective-permute-start(bf16[128,4096]{1,0:T(8,128)(2,1)} %bitcast.29), channel_id=1, source_target_pairs={{0,256},{256,0},{16,272},{272,16},{32,288},{288,32},{48,304},{304,... | collective-permute-start | bytes 3145736 | tf_op jit(solution)/shard_map/ppermute | solution.py:228
  6.3 0.0 copy-start
  6.3 3.5 %own_gradient.1 = bf16[16,32,128]{2,1,0:T(8,128)(2,1)S(1)} custom-call(bf16[128,4096]{1,0:T(8,128)(2,1)} %bitcast.32, bf16[128,4096]{1,0:T(8,128)(2,1)} %bitcast.33, s32[1]{0:T(128)S(6)} %copy.19.n_hbm, bf16[64,4096]{1,0:T(8,128)(2,1)} %bitcast.35, bf16[64,4096]{1,0:T(8,128)(2,1)} %bitcast.36, f32[64,64]{1,0:T(8,128)} %bitcast.39, f32[64,64]{1,0:T(8,128)} %bitcast.40), custom_call_target="tpu_custom_call" | custom-call | tf_op jit(solution)/shard_map/own_gradient/pallas_call | solution.py:64
  9.8 19.0 %all_to_all.10 = bf16[16,32,128]{2,1,0:T(8,128)(2,1)S(1)} all-to-all(bf16[16,32,128]{2,1,0:T(8,128)(2,1)S(1)} %own_gradient.1), channel_id=1, replica_groups={{128,144,160,176,0,16,32,48,192,208,224,240,64,80,96,112},{129,145,161,..., dimensions={0} | all-to-all | bytes 262144 | tf_op jit(solution)/shard_map/all_to_all | solution.py:122
  28.8 0.0 collective-permute-done.yh_ref
  28.8 0.7 %collective-permute-start.2 = (bf16[16,32,128]{2,1,0:T(8,128)(2,1)S(1)}, bf16[16,32,128]{2,1,0:T(8,128)(2,1)S(1)}, u32[]{:S(2)}, u32[]{:S(2)}) collective-permute-start(bf16[16,32,128]{2,1,0:T(8,128)(2,1)S(1)} %all_to_all.10), channel_id=1, source_target_pairs={{112,368},{368,112},{128,384},{384,128},{144,400},{400,144},{160,4... | collective-permute-start | bytes 393224 | tf_op jit(solution)/shard_map/ppermute | solution.py:230
  29.5 4.4 %collective-permute-start.1 = (bf16[16,32,128]{2,1,0:T(8,128)(2,1)S(1)}, bf16[16,32,128]{2,1,0:T(8,128)(2,1)S(1)}, u32[]{:S(2)}, u32[]{:S(2)}) collective-permute-start(bf16[16,32,128]{2,1,0:T(8,128)(2,1)S(1)} %all_to_all.10), channel_id=1, source_target_pairs={{0,8},{8,0},{16,24},{24,16},{32,40},{40,32},{48,56},{56,48},{64,72... | collective-permute-start | bytes 393224 | tf_op jit(solution)/shard_map/ppermute | solution.py:231
  33.9 0.0 copy-done
  33.9 0.7 %collective-permute-start.3 = (bf16[128,4096]{1,0:T(8,128)(2,1)S(1)}, bf16[128,4096]{1,0:T(8,128)(2,1)S(1)}, u32[]{:S(2)}, u32[]{:S(2)}) collective-permute-start(bf16[128,4096]{1,0:T(8,128)(2,1)S(1)} %bitcast.30), channel_id=1, source_target_pairs={{112,120},{120,112},{128,136},{136,128},{144,152},{152,144},{160,1... | collective-permute-start | bytes 3145736 | tf_op jit(solution)/shard_map/ppermute | solution.py:232
  34.6 0.1 copy.18
  34.7 0.0 collective-permute-done.2
  34.7 0.1 copy.16
  34.7 0.1 collective-permute-done.1
  34.8 0.1 copy.17
  34.9 0.5 scored_mine.1.mine_s
  35.3 0.0 collective-permute-done.3.core_ref
  35.4 0.5 scored.1
  35.9 12.7 %all_to_all.11 = f32[32,8,128]{2,1,0:T(8,128)S(1)} all-to-all(f32[32,8,128]{2,1,0:T(8,128)S(1)} %scored.1), channel_id=1, replica_groups={{271,0,1,2,3,4,5,6,7,8,9,10,11,12,13,14,15,256,257,258,259,260,261,262,..., dimensions={0} | all-to-all | bytes 262144 | tf_op jit(solution)/shard_map/all_to_all | solution.py:235
  48.6 0.6 %copy.9 = f32[4,2,128]{2,1,0:T(2,128)} copy(f32[4,2,128]{2,0,1:T(4,128)S(1)} %bitcast.41) | data formatting | bytes 8192 | tf_op jit(solution)/shard_map/transpose | solution.py:239
  (1 shorter events, 0.0 us)
Async XLA Ops:
  0.0 28.8 %collective-permute-start = (bf16[128,4096]{1,0:T(8,128)(2,1)}, bf16[128,4096]{1,0:T(8,128)(2,1)S(1)}, u32[]{:S(2)}, u32[]{:S(2)}) collective-permute-start(bf16[128,4096]{1,0:T(8,128)(2,1)} %bitcast.29), channel_id=1, source_target_pairs={{0,256},{256,0},{16,272},{272,16},{32,288},{288,32},{48,304},{304,... | collective-permute-start | bytes 3145736 | tf_op jit(solution)/shard_map/ppermute | solution.py:228
  6.3 27.6 %copy-start = (bf16[1,128,4096]{2,1,0:T(8,128)(2,1)S(1)}, bf16[1,128,4096]{2,1,0:T(8,128)(2,1)}, u32[]{:S(2)}) copy-start(bf16[1,128,4096]{2,1,0:T(8,128)(2,1)} %param.15) | copy-start | bytes 3145732
  28.8 5.9 %collective-permute-start.2 = (bf16[16,32,128]{2,1,0:T(8,128)(2,1)S(1)}, bf16[16,32,128]{2,1,0:T(8,128)(2,1)S(1)}, u32[]{:S(2)}, u32[]{:S(2)}) collective-permute-start(bf16[16,32,128]{2,1,0:T(8,128)(2,1)S(1)} %all_to_all.10), channel_id=1, source_target_pairs={{112,368},{368,112},{128,384},{384,128},{144,400},{400,144},{160,4... | collective-permute-start | bytes 393224 | tf_op jit(solution)/shard_map/ppermute | solution.py:230
  29.5 5.4 %collective-permute-start.1 = (bf16[16,32,128]{2,1,0:T(8,128)(2,1)S(1)}, bf16[16,32,128]{2,1,0:T(8,128)(2,1)S(1)}, u32[]{:S(2)}, u32[]{:S(2)}) collective-permute-start(bf16[16,32,128]{2,1,0:T(8,128)(2,1)S(1)} %all_to_all.10), channel_id=1, source_target_pairs={{0,8},{8,0},{16,24},{24,16},{32,40},{40,32},{48,56},{56,48},{64,72... | collective-permute-start | bytes 393224 | tf_op jit(solution)/shard_map/ppermute | solution.py:231
  33.9 1.5 %collective-permute-start.3 = (bf16[128,4096]{1,0:T(8,128)(2,1)S(1)}, bf16[128,4096]{1,0:T(8,128)(2,1)S(1)}, u32[]{:S(2)}, u32[]{:S(2)}) collective-permute-start(bf16[128,4096]{1,0:T(8,128)(2,1)S(1)} %bitcast.30), channel_id=1, source_target_pairs={{112,120},{120,112},{128,136},{136,128},{144,152},{152,144},{160,1... | collective-permute-start | bytes 3145736 | tf_op jit(solution)/shard_map/ppermute | solution.py:232

commit v6 on v5

--- a/solution.py
+++ b/solution.py
@@ -90,7 +90,7 @@
 
 def runs_of(places):
     half = places // RUN // 2
-    return [r for i in range(half) for r in (half + i, i)]
+    return [half, *range(half), *range(half + 1, 2 * half)]
 
 
 def pairs(planes, places):
@@ -166,7 +166,7 @@
         other_s[...] = lax.dot_general(q, other_ref[...], nt, preferred_element_type=jnp.float32)
 
     def put(h, c, layer, first, second):
-        rows = jnp.concatenate([first, second], axis=0)
+        rows = jnp.concatenate([first, second], axis=0).astype(o_ref.dtype)
         o_ref[lax.rem((h * CORES + c) * layers + layer + 1, blocks)] = rows
 
     @pl.when(z < EARLY)
@@ -196,7 +196,7 @@
     vmem = pl.BlockSpec(memory_space=pltpu.VMEM)
     return pl.pallas_call(
         functools.partial(_score_kernel, places),
-        out_shape=jax.ShapeDtypeStruct((Y_HI * CORES * layers, CORES * RUN, train), jnp.float32),
+        out_shape=jax.ShapeDtypeStruct((Y_HI * CORES * layers, CORES * RUN, train), jnp.bfloat16),
         in_specs=[vmem] * 6,
         out_specs=vmem,
         scratch_shapes=[pltpu.VMEM((2 * places, train), jnp.float32)],
@@ -235,7 +235,7 @@
     terms = lax.all_to_all(
         parts, ("yh", "core", "x", "yl"), 0, 0, axis_index_groups=last_first(parts.shape[0])
     )
-    terms = jnp.sum(terms, axis=0)
+    terms = jnp.sum(terms.astype(jnp.float32), axis=0)
     return terms.reshape(CORES, RUN, train).transpose(1, 0, 2).reshape(-1, train)
 
 

time: 49.7 us -> 49.3 us (level)
  starting transfers between devices: 11.4 us -> 10.6 us
  blocking collectives: 31.7 us -> 32.4 us
    all_to_all x1, blocking collectives: 19 us -> 20 us  [gathered(): return lax.all_to_all(sent, 'z', 0, 0, axis_index_groups=[order])]
    ppermute x1, starting transfers between devices: 4.4 us -> 3.62 us  [body(): core_queries = lax.ppermute(held, ('z', 'core'), early_core)]
where the time goes in v6:
time: 49.3 us; the launch traced here: 49.1 us
  blocking collectives  32.4 us (66%)
  starting transfers between devices  10.6 us (22%)
  Pallas kernels  4.42 us (9%)
  local copies, waits for them, and re-layouts  0.77 us (2%)
  between operations  0.74 us (2%)
    all_to_all x1, blocking collectives, gathered(): return lax.all_to_all(sent, 'z', 0, 0, axis_index_groups=[order])  20 us
    all_to_all x1, blocking collectives, body(): lax.all_to_all(parts, ('yh', 'core', 'x', 'yl'), 0, 0, axis_index_groups=...  12.4 us
    ppermute x1, starting transfers between devices, body(): yh_rows = lax.ppermute(mine, ('yh', 'z'), early_yh)  5.64 us
    ppermute x1, starting transfers between devices, body(): core_queries = lax.ppermute(held, ('z', 'core'), early_core)  3.62 us
    pallas_call x1, Pallas kernels, own_gradient(): pl.pallas_call(functools.partial(_own_kernel, copies), out_shape=jax.Shap...  3.49 us
  transfers between devices with their start and end apart: 4, of which 1 were waited for; matrix products, arithmetic and copies ran while one was open for 0% of the time, Pallas kernels for 8%

profile of v6, /device:TPU:1, one launch (start us, length us, event | category | flops | bytes accessed | tf_op | source)
XLA Modules:
  0.0 49.1 jit_solution(15225829040964750768)
XLA Ops:
  0.0 5.6 %collective-permute-start = (bf16[128,4096]{1,0:T(8,128)(2,1)}, bf16[128,4096]{1,0:T(8,128)(2,1)S(1)}, u32[]{:S(2)}, u32[]{:S(2)}) collective-permute-start(bf16[128,4096]{1,0:T(8,128)(2,1)} %bitcast.29), channel_id=1, source_target_pairs={{0,256},{256,0},{16,272},{272,16},{32,288},{288,32},{48,304},{304,... | collective-permute-start | bytes 3145736 | tf_op jit(solution)/shard_map/ppermute | solution.py:228
  6.3 0.0 copy-start
  6.3 3.5 %own_gradient.1 = bf16[16,32,128]{2,1,0:T(8,128)(2,1)S(1)} custom-call(bf16[128,4096]{1,0:T(8,128)(2,1)} %bitcast.32, bf16[128,4096]{1,0:T(8,128)(2,1)} %bitcast.33, s32[1]{0:T(128)S(6)} %copy.19.n_hbm, bf16[64,4096]{1,0:T(8,128)(2,1)} %bitcast.35, bf16[64,4096]{1,0:T(8,128)(2,1)} %bitcast.36, f32[64,64]{1,0:T(8,128)} %bitcast.39, f32[64,64]{1,0:T(8,128)} %bitcast.40), custom_call_target="tpu_custom_call" | custom-call | tf_op jit(solution)/shard_map/own_gradient/pallas_call | solution.py:64
  9.8 20.0 %all_to_all.10 = bf16[16,32,128]{2,1,0:T(8,128)(2,1)S(1)} all-to-all(bf16[16,32,128]{2,1,0:T(8,128)(2,1)S(1)} %own_gradient.1), channel_id=1, replica_groups={{128,144,160,176,0,16,32,48,64,80,96,112,192,208,224,240},{129,145,161,..., dimensions={0} | all-to-all | bytes 262144 | tf_op jit(solution)/shard_map/all_to_all | solution.py:122
  29.8 0.0 collective-permute-done.yh_ref
  29.8 0.7 %collective-permute-start.2 = (bf16[16,32,128]{2,1,0:T(8,128)(2,1)S(1)}, bf16[16,32,128]{2,1,0:T(8,128)(2,1)S(1)}, u32[]{:S(2)}, u32[]{:S(2)}) collective-permute-start(bf16[16,32,128]{2,1,0:T(8,128)(2,1)S(1)} %all_to_all.10), channel_id=1, source_target_pairs={{112,368},{368,112},{128,384},{384,128},{144,400},{400,144},{160,4... | collective-permute-start | bytes 393224 | tf_op jit(solution)/shard_map/ppermute | solution.py:230
  30.5 3.6 %collective-permute-start.1 = (bf16[16,32,128]{2,1,0:T(8,128)(2,1)S(1)}, bf16[16,32,128]{2,1,0:T(8,128)(2,1)S(1)}, u32[]{:S(2)}, u32[]{:S(2)}) collective-permute-start(bf16[16,32,128]{2,1,0:T(8,128)(2,1)S(1)} %all_to_all.10), channel_id=1, source_target_pairs={{0,8},{8,0},{16,24},{24,16},{32,40},{40,32},{48,56},{56,48},{64,72... | collective-permute-start | bytes 393224 | tf_op jit(solution)/shard_map/ppermute | solution.py:231
  34.1 0.0 copy-done
  34.1 0.7 %collective-permute-start.3 = (bf16[128,4096]{1,0:T(8,128)(2,1)S(1)}, bf16[128,4096]{1,0:T(8,128)(2,1)S(1)}, u32[]{:S(2)}, u32[]{:S(2)}) collective-permute-start(bf16[128,4096]{1,0:T(8,128)(2,1)S(1)} %bitcast.30), channel_id=1, source_target_pairs={{112,120},{120,112},{128,136},{136,128},{144,152},{152,144},{160,1... | collective-permute-start | bytes 3145736 | tf_op jit(solution)/shard_map/ppermute | solution.py:232
  34.9 0.1 copy.18
  34.9 0.0 collective-permute-done.2
  34.9 0.1 copy.16
  35.0 0.1 collective-permute-done.1
  35.1 0.1 copy.17
  35.1 0.5 scored_mine.1.mine_s
  35.6 0.0 collective-permute-done.3.core_ref
  35.6 0.5 scored.1
  36.1 12.4 %all_to_all.11 = bf16[32,8,128]{2,1,0:T(8,128)(2,1)S(1)} all-to-all(bf16[32,8,128]{2,1,0:T(8,128)(2,1)S(1)} %scored.1), channel_id=1, replica_groups={{271,0,1,2,3,4,5,6,7,8,9,10,11,12,13,14,15,256,257,258,259,260,261,262,..., dimensions={0} | all-to-all | bytes 131072 | tf_op jit(solution)/shard_map/all_to_all | solution.py:235
  48.5 0.6 %copy.9 = f32[4,2,128]{2,1,0:T(2,128)} copy(f32[4,2,128]{2,0,1:T(4,128)S(1)} %bitcast.41) | data formatting | bytes 8192 | tf_op jit(solution)/shard_map/transpose | solution.py:239
  (1 shorter events, 0.0 us)
Async XLA Ops:
  0.0 29.8 %collective-permute-start = (bf16[128,4096]{1,0:T(8,128)(2,1)}, bf16[128,4096]{1,0:T(8,128)(2,1)S(1)}, u32[]{:S(2)}, u32[]{:S(2)}) collective-permute-start(bf16[128,4096]{1,0:T(8,128)(2,1)} %bitcast.29), channel_id=1, source_target_pairs={{0,256},{256,0},{16,272},{272,16},{32,288},{288,32},{48,304},{304,... | collective-permute-start | bytes 3145736 | tf_op jit(solution)/shard_map/ppermute | solution.py:228
  6.3 27.8 %copy-start = (bf16[1,128,4096]{2,1,0:T(8,128)(2,1)S(1)}, bf16[1,128,4096]{2,1,0:T(8,128)(2,1)}, u32[]{:S(2)}) copy-start(bf16[1,128,4096]{2,1,0:T(8,128)(2,1)} %param.15) | copy-start | bytes 3145732
  29.8 5.1 %collective-permute-start.2 = (bf16[16,32,128]{2,1,0:T(8,128)(2,1)S(1)}, bf16[16,32,128]{2,1,0:T(8,128)(2,1)S(1)}, u32[]{:S(2)}, u32[]{:S(2)}) collective-permute-start(bf16[16,32,128]{2,1,0:T(8,128)(2,1)S(1)} %all_to_all.10), channel_id=1, source_target_pairs={{112,368},{368,112},{128,384},{384,128},{144,400},{400,144},{160,4... | collective-permute-start | bytes 393224 | tf_op jit(solution)/shard_map/ppermute | solution.py:230
  30.5 4.6 %collective-permute-start.1 = (bf16[16,32,128]{2,1,0:T(8,128)(2,1)S(1)}, bf16[16,32,128]{2,1,0:T(8,128)(2,1)S(1)}, u32[]{:S(2)}, u32[]{:S(2)}) collective-permute-start(bf16[16,32,128]{2,1,0:T(8,128)(2,1)S(1)} %all_to_all.10), channel_id=1, source_target_pairs={{0,8},{8,0},{16,24},{24,16},{32,40},{40,32},{48,56},{56,48},{64,72... | collective-permute-start | bytes 393224 | tf_op jit(solution)/shard_map/ppermute | solution.py:231
  34.1 1.5 %collective-permute-start.3 = (bf16[128,4096]{1,0:T(8,128)(2,1)S(1)}, bf16[128,4096]{1,0:T(8,128)(2,1)S(1)}, u32[]{:S(2)}, u32[]{:S(2)}) collective-permute-start(bf16[128,4096]{1,0:T(8,128)(2,1)S(1)} %bitcast.30), channel_id=1, source_target_pairs={{112,120},{120,112},{128,136},{136,128},{144,152},{152,144},{160,1... | collective-permute-start | bytes 3145736 | tf_op jit(solution)/shard_map/ppermute | solution.py:232

commit v7 on v6

--- a/solution.py
+++ b/solution.py
@@ -88,9 +88,16 @@
 EARLY = 7
 
 
-def runs_of(places):
-    half = places // RUN // 2
-    return [half, *range(half), *range(half + 1, 2 * half)]
+def order_of(places):
+    half = places // 2
+    near, far = list(range(RUN)), list(range(half + 1, half + RUN))
+    return [half, *near, *far, *range(RUN, half), *range(half + RUN, places)]
+
+
+def run_at(rows, first, layer, places):
+    order = order_of(places)
+    at = [first + order.index(layer * RUN + i) for i in range(RUN)]
+    return jnp.concatenate([rows[a : a + 1] for a in at], axis=0)
 
 
 def pairs(planes, places):
@@ -118,7 +125,7 @@
 
 def gathered(sent):
     places = lax.axis_size("z")
-    order = [r * RUN + i for r in runs_of(places) for i in range(RUN)]
+    order = order_of(places)
     return lax.all_to_all(sent, "z", 0, 0, axis_index_groups=[order])
 
 
@@ -158,7 +165,7 @@
     yh, core, z = lax.axis_index("yh"), lax.axis_index("core"), lax.axis_index("z")
     blocks = o_ref.shape[0]
     layers = blocks // (Y_HI * CORES)
-    runs = runs_of(places)
+    runs = places // RUN
     o_ref[...] = jnp.zeros(o_ref.shape, o_ref.dtype)
 
     def score(more_ref, other_ref):
@@ -173,22 +180,20 @@
     def _():
         score(core_q_ref, yh_ref)
         for s, h in ((mine_s, yh), (other_s, 1 - yh)):
-            for i, r in enumerate(runs):
-                own = s[i * RUN : (i + 1) * RUN]
-                more = s[places + i * RUN : places + (i + 1) * RUN]
+            for r in range(runs):
+                own, more = (run_at(s[...], first, r, places) for first in (0, places))
                 first = jnp.where(core == 0, own, more)
-                put(h, core, yh * len(runs) + r, first, jnp.where(core == 0, more, own))
+                put(h, core, yh * runs + r, first, jnp.where(core == 0, more, own))
 
     @pl.when(z >= EARLY)
     def _():
         score(yh_q_ref, core_ref)
         for s, c in ((mine_s, core), (other_s, 1 - core)):
             for half, h in ((0, yh), (1, 1 - yh)):
-                for i, r in enumerate(runs):
-                    at = half * places + i * RUN
-                    own = s[at : at + RUN]
+                for r in range(runs):
+                    own = run_at(s[...], half * places, r, places)
                     none = jnp.zeros_like(own)
-                    put(yh, c, h * len(runs) + r, jnp.where(core == 0, own, none), jnp.where(core == 0, none, own))
+                    put(yh, c, h * runs + r, jnp.where(core == 0, own, none), jnp.where(core == 0, none, own))
 
 
 def scored(places, layers, *operands):

time: 49.3 us -> 49.4 us (level)
  no operation moved by 1% of the time
where the time goes in v7:
time: 49.4 us; the launch traced here: 49.1 us
  blocking collectives  32.3 us (65%)
  starting transfers between devices  10.7 us (22%)
  Pallas kernels  4.42 us (9%)
  local copies, waits for them, and re-layouts  0.77 us (2%)
  between operations  0.74 us (1%)
    all_to_all x1, blocking collectives, gathered(): return lax.all_to_all(sent, 'z', 0, 0, axis_index_groups=[order])  19.9 us
    all_to_all x1, blocking collectives, body(): lax.all_to_all(parts, ('yh', 'core', 'x', 'yl'), 0, 0, axis_index_groups=...  12.4 us
    ppermute x1, starting transfers between devices, body(): yh_rows = lax.ppermute(mine, ('yh', 'z'), early_yh)  5.64 us
    ppermute x1, starting transfers between devices, body(): core_queries = lax.ppermute(held, ('z', 'core'), early_core)  3.7 us
    pallas_call x1, Pallas kernels, own_gradient(): pl.pallas_call(functools.partial(_own_kernel, copies), out_shape=jax.Shap...  3.49 us
  transfers between devices with their start and end apart: 4, of which 1 were waited for; matrix products, arithmetic and copies ran while one was open for 0% of the time, Pallas kernels for 8%

profile of v7, /device:TPU:1, one launch (start us, length us, event | category | flops | bytes accessed | tf_op | source)
XLA Modules:
  0.0 49.1 jit_solution(2134364961618633652)
XLA Ops:
  0.0 5.6 %collective-permute-start = (bf16[128,4096]{1,0:T(8,128)(2,1)}, bf16[128,4096]{1,0:T(8,128)(2,1)S(1)}, u32[]{:S(2)}, u32[]{:S(2)}) collective-permute-start(bf16[128,4096]{1,0:T(8,128)(2,1)} %bitcast.29), channel_id=1, source_target_pairs={{0,256},{256,0},{16,272},{272,16},{32,288},{288,32},{48,304},{304,... | collective-permute-start | bytes 3145736 | tf_op jit(solution)/shard_map/ppermute | solution.py:233
  6.3 0.0 copy-start
  6.3 3.5 %own_gradient.1 = bf16[16,32,128]{2,1,0:T(8,128)(2,1)S(1)} custom-call(bf16[128,4096]{1,0:T(8,128)(2,1)} %bitcast.32, bf16[128,4096]{1,0:T(8,128)(2,1)} %bitcast.33, s32[1]{0:T(128)S(6)} %copy.19.n_hbm, bf16[64,4096]{1,0:T(8,128)(2,1)} %bitcast.35, bf16[64,4096]{1,0:T(8,128)(2,1)} %bitcast.36, f32[64,64]{1,0:T(8,128)} %bitcast.39, f32[64,64]{1,0:T(8,128)} %bitcast.40), custom_call_target="tpu_custom_call" | custom-call | tf_op jit(solution)/shard_map/own_gradient/pallas_call | solution.py:64
  9.8 19.9 %all_to_all.10 = bf16[16,32,128]{2,1,0:T(8,128)(2,1)S(1)} all-to-all(bf16[16,32,128]{2,1,0:T(8,128)(2,1)S(1)} %own_gradient.1), channel_id=1, replica_groups={{128,0,16,32,48,144,160,176,64,80,96,112,192,208,224,240},{129,1,17,33,..., dimensions={0} | all-to-all | bytes 262144 | tf_op jit(solution)/shard_map/all_to_all | solution.py:129
  29.7 0.0 collective-permute-done.yh_ref
  29.7 0.7 %collective-permute-start.2 = (bf16[16,32,128]{2,1,0:T(8,128)(2,1)S(1)}, bf16[16,32,128]{2,1,0:T(8,128)(2,1)S(1)}, u32[]{:S(2)}, u32[]{:S(2)}) collective-permute-start(bf16[16,32,128]{2,1,0:T(8,128)(2,1)S(1)} %all_to_all.10), channel_id=1, source_target_pairs={{112,368},{368,112},{128,384},{384,128},{144,400},{400,144},{160,4... | collective-permute-start | bytes 393224 | tf_op jit(solution)/shard_map/ppermute | solution.py:235
  30.4 3.7 %collective-permute-start.1 = (bf16[16,32,128]{2,1,0:T(8,128)(2,1)S(1)}, bf16[16,32,128]{2,1,0:T(8,128)(2,1)S(1)}, u32[]{:S(2)}, u32[]{:S(2)}) collective-permute-start(bf16[16,32,128]{2,1,0:T(8,128)(2,1)S(1)} %all_to_all.10), channel_id=1, source_target_pairs={{0,8},{8,0},{16,24},{24,16},{32,40},{40,32},{48,56},{56,48},{64,72... | collective-permute-start | bytes 393224 | tf_op jit(solution)/shard_map/ppermute | solution.py:236
  34.1 0.0 copy-done
  34.1 0.7 %collective-permute-start.3 = (bf16[128,4096]{1,0:T(8,128)(2,1)S(1)}, bf16[128,4096]{1,0:T(8,128)(2,1)S(1)}, u32[]{:S(2)}, u32[]{:S(2)}) collective-permute-start(bf16[128,4096]{1,0:T(8,128)(2,1)S(1)} %bitcast.30), channel_id=1, source_target_pairs={{112,120},{120,112},{128,136},{136,128},{144,152},{152,144},{160,1... | collective-permute-start | bytes 3145736 | tf_op jit(solution)/shard_map/ppermute | solution.py:237
  34.9 0.1 copy.18
  34.9 0.0 collective-permute-done.2
  34.9 0.1 copy.16
  35.0 0.1 collective-permute-done.1
  35.1 0.1 copy.17
  35.1 0.5 scored_mine.1.mine_s
  35.6 0.0 collective-permute-done.3.core_ref
  35.6 0.5 scored.1
  36.1 12.4 %all_to_all.11 = bf16[32,8,128]{2,1,0:T(8,128)(2,1)S(1)} all-to-all(bf16[32,8,128]{2,1,0:T(8,128)(2,1)S(1)} %scored.1), channel_id=1, replica_groups={{271,0,1,2,3,4,5,6,7,8,9,10,11,12,13,14,15,256,257,258,259,260,261,262,..., dimensions={0} | all-to-all | bytes 131072 | tf_op jit(solution)/shard_map/all_to_all | solution.py:240
  48.5 0.6 %copy.9 = f32[4,2,128]{2,1,0:T(2,128)} copy(f32[4,2,128]{2,0,1:T(4,128)S(1)} %bitcast.41) | data formatting | bytes 8192 | tf_op jit(solution)/shard_map/transpose | solution.py:244
  (1 shorter events, 0.0 us)
Async XLA Ops:
  0.0 29.7 %collective-permute-start = (bf16[128,4096]{1,0:T(8,128)(2,1)}, bf16[128,4096]{1,0:T(8,128)(2,1)S(1)}, u32[]{:S(2)}, u32[]{:S(2)}) collective-permute-start(bf16[128,4096]{1,0:T(8,128)(2,1)} %bitcast.29), channel_id=1, source_target_pairs={{0,256},{256,0},{16,272},{272,16},{32,288},{288,32},{48,304},{304,... | collective-permute-start | bytes 3145736 | tf_op jit(solution)/shard_map/ppermute | solution.py:233
  6.3 27.8 %copy-start = (bf16[1,128,4096]{2,1,0:T(8,128)(2,1)S(1)}, bf16[1,128,4096]{2,1,0:T(8,128)(2,1)}, u32[]{:S(2)}) copy-start(bf16[1,128,4096]{2,1,0:T(8,128)(2,1)} %param.15) | copy-start | bytes 3145732
  29.7 5.2 %collective-permute-start.2 = (bf16[16,32,128]{2,1,0:T(8,128)(2,1)S(1)}, bf16[16,32,128]{2,1,0:T(8,128)(2,1)S(1)}, u32[]{:S(2)}, u32[]{:S(2)}) collective-permute-start(bf16[16,32,128]{2,1,0:T(8,128)(2,1)S(1)} %all_to_all.10), channel_id=1, source_target_pairs={{112,368},{368,112},{128,384},{384,128},{144,400},{400,144},{160,4... | collective-permute-start | bytes 393224 | tf_op jit(solution)/shard_map/ppermute | solution.py:235
  30.4 4.7 %collective-permute-start.1 = (bf16[16,32,128]{2,1,0:T(8,128)(2,1)S(1)}, bf16[16,32,128]{2,1,0:T(8,128)(2,1)S(1)}, u32[]{:S(2)}, u32[]{:S(2)}) collective-permute-start(bf16[16,32,128]{2,1,0:T(8,128)(2,1)S(1)} %all_to_all.10), channel_id=1, source_target_pairs={{0,8},{8,0},{16,24},{24,16},{32,40},{40,32},{48,56},{56,48},{64,72... | collective-permute-start | bytes 393224 | tf_op jit(solution)/shard_map/ppermute | solution.py:236
  34.1 1.5 %collective-permute-start.3 = (bf16[128,4096]{1,0:T(8,128)(2,1)S(1)}, bf16[128,4096]{1,0:T(8,128)(2,1)S(1)}, u32[]{:S(2)}, u32[]{:S(2)}) collective-permute-start(bf16[128,4096]{1,0:T(8,128)(2,1)S(1)} %bitcast.30), channel_id=1, source_target_pairs={{112,120},{120,112},{128,136},{136,128},{144,152},{152,144},{160,1... | collective-permute-start | bytes 3145736 | tf_op jit(solution)/shard_map/ppermute | solution.py:237

commit v8 on v6

--- a/solution.py
+++ b/solution.py
@@ -90,7 +90,7 @@
 
 def runs_of(places):
     half = places // RUN // 2
-    return [half, *range(half), *range(half + 1, 2 * half)]
+    return [r for i in range(half) for r in (half + i, i)]
 
 
 def pairs(planes, places):

time: 49.3 us -> 49.4 us (level)
  blocking collectives: 32.4 us -> 31.3 us
  starting transfers between devices: 10.6 us -> 11.4 us
    all_to_all x1, blocking collectives: 20 us -> 19 us  [gathered(): return lax.all_to_all(sent, 'z', 0, 0, axis_index_groups=[order])]
    ppermute x1, starting transfers between devices: 3.62 us -> 4.4 us  [body(): core_queries = lax.ppermute(held, ('z', 'core'), early_core)]
where the time goes in v8:
time: 49.4 us; the launch traced here: 48.8 us
  blocking collectives  31.3 us (63%)
  starting transfers between devices  11.4 us (23%)
  Pallas kernels  4.42 us (9%)
  local copies, waits for them, and re-layouts  0.77 us (2%)
  between operations  0.74 us (1%)
    all_to_all x1, blocking collectives, gathered(): return lax.all_to_all(sent, 'z', 0, 0, axis_index_groups=[order])  19 us
    all_to_all x1, blocking collectives, body(): lax.all_to_all(parts, ('yh', 'core', 'x', 'yl'), 0, 0, axis_index_groups=...  12.4 us
    ppermute x1, starting transfers between devices, body(): yh_rows = lax.ppermute(mine, ('yh', 'z'), early_yh)  5.64 us
    ppermute x1, starting transfers between devices, body(): core_queries = lax.ppermute(held, ('z', 'core'), early_core)  4.4 us
    pallas_call x1, Pallas kernels, own_gradient(): pl.pallas_call(functools.partial(_own_kernel, copies), out_shape=jax.Shap...  3.49 us
  transfers between devices with their start and end apart: 4, of which 1 were waited for; matrix products, arithmetic and copies ran while one was open for 0% of the time, Pallas kernels for 8%

profile of v8, /device:TPU:1, one launch (start us, length us, event | category | flops | bytes accessed | tf_op | source)
XLA Modules:
  0.0 48.8 jit_solution(1396021571497499432)
XLA Ops:
  0.0 5.6 %collective-permute-start = (bf16[128,4096]{1,0:T(8,128)(2,1)}, bf16[128,4096]{1,0:T(8,128)(2,1)S(1)}, u32[]{:S(2)}, u32[]{:S(2)}) collective-permute-start(bf16[128,4096]{1,0:T(8,128)(2,1)} %bitcast.29), channel_id=1, source_target_pairs={{0,256},{256,0},{16,272},{272,16},{32,288},{288,32},{48,304},{304,... | collective-permute-start | bytes 3145736 | tf_op jit(solution)/shard_map/ppermute | solution.py:228
  6.3 0.0 copy-start
  6.3 3.5 %own_gradient.1 = bf16[16,32,128]{2,1,0:T(8,128)(2,1)S(1)} custom-call(bf16[128,4096]{1,0:T(8,128)(2,1)} %bitcast.32, bf16[128,4096]{1,0:T(8,128)(2,1)} %bitcast.33, s32[1]{0:T(128)S(6)} %copy.19.n_hbm, bf16[64,4096]{1,0:T(8,128)(2,1)} %bitcast.35, bf16[64,4096]{1,0:T(8,128)(2,1)} %bitcast.36, f32[64,64]{1,0:T(8,128)} %bitcast.39, f32[64,64]{1,0:T(8,128)} %bitcast.40), custom_call_target="tpu_custom_call" | custom-call | tf_op jit(solution)/shard_map/own_gradient/pallas_call | solution.py:64
  9.8 19.0 %all_to_all.10 = bf16[16,32,128]{2,1,0:T(8,128)(2,1)S(1)} all-to-all(bf16[16,32,128]{2,1,0:T(8,128)(2,1)S(1)} %own_gradient.1), channel_id=1, replica_groups={{128,144,160,176,0,16,32,48,192,208,224,240,64,80,96,112},{129,145,161,..., dimensions={0} | all-to-all | bytes 262144 | tf_op jit(solution)/shard_map/all_to_all | solution.py:122
  28.8 0.0 collective-permute-done.yh_ref
  28.8 0.7 %collective-permute-start.2 = (bf16[16,32,128]{2,1,0:T(8,128)(2,1)S(1)}, bf16[16,32,128]{2,1,0:T(8,128)(2,1)S(1)}, u32[]{:S(2)}, u32[]{:S(2)}) collective-permute-start(bf16[16,32,128]{2,1,0:T(8,128)(2,1)S(1)} %all_to_all.10), channel_id=1, source_target_pairs={{112,368},{368,112},{128,384},{384,128},{144,400},{400,144},{160,4... | collective-permute-start | bytes 393224 | tf_op jit(solution)/shard_map/ppermute | solution.py:230
  29.5 4.4 %collective-permute-start.1 = (bf16[16,32,128]{2,1,0:T(8,128)(2,1)S(1)}, bf16[16,32,128]{2,1,0:T(8,128)(2,1)S(1)}, u32[]{:S(2)}, u32[]{:S(2)}) collective-permute-start(bf16[16,32,128]{2,1,0:T(8,128)(2,1)S(1)} %all_to_all.10), channel_id=1, source_target_pairs={{0,8},{8,0},{16,24},{24,16},{32,40},{40,32},{48,56},{56,48},{64,72... | collective-permute-start | bytes 393224 | tf_op jit(solution)/shard_map/ppermute | solution.py:231
  33.9 0.0 copy-done
  33.9 0.7 %collective-permute-start.3 = (bf16[128,4096]{1,0:T(8,128)(2,1)S(1)}, bf16[128,4096]{1,0:T(8,128)(2,1)S(1)}, u32[]{:S(2)}, u32[]{:S(2)}) collective-permute-start(bf16[128,4096]{1,0:T(8,128)(2,1)S(1)} %bitcast.30), channel_id=1, source_target_pairs={{112,120},{120,112},{128,136},{136,128},{144,152},{152,144},{160,1... | collective-permute-start | bytes 3145736 | tf_op jit(solution)/shard_map/ppermute | solution.py:232
  34.6 0.1 copy.18
  34.7 0.0 collective-permute-done.2
  34.7 0.1 copy.16
  34.7 0.1 collective-permute-done.1
  34.8 0.1 copy.17
  34.9 0.5 scored_mine.1.mine_s
  35.3 0.0 collective-permute-done.3.core_ref
  35.4 0.5 scored.1
  35.9 12.4 %all_to_all.11 = bf16[32,8,128]{2,1,0:T(8,128)(2,1)S(1)} all-to-all(bf16[32,8,128]{2,1,0:T(8,128)(2,1)S(1)} %scored.1), channel_id=1, replica_groups={{271,0,1,2,3,4,5,6,7,8,9,10,11,12,13,14,15,256,257,258,259,260,261,262,..., dimensions={0} | all-to-all | bytes 131072 | tf_op jit(solution)/shard_map/all_to_all | solution.py:235
  48.2 0.6 %copy.9 = f32[4,2,128]{2,1,0:T(2,128)} copy(f32[4,2,128]{2,0,1:T(4,128)S(1)} %bitcast.41) | data formatting | bytes 8192 | tf_op jit(solution)/shard_map/transpose | solution.py:239
  (1 shorter events, 0.0 us)
Async XLA Ops:
  0.0 28.8 %collective-permute-start = (bf16[128,4096]{1,0:T(8,128)(2,1)}, bf16[128,4096]{1,0:T(8,128)(2,1)S(1)}, u32[]{:S(2)}, u32[]{:S(2)}) collective-permute-start(bf16[128,4096]{1,0:T(8,128)(2,1)} %bitcast.29), channel_id=1, source_target_pairs={{0,256},{256,0},{16,272},{272,16},{32,288},{288,32},{48,304},{304,... | collective-permute-start | bytes 3145736 | tf_op jit(solution)/shard_map/ppermute | solution.py:228
  6.3 27.6 %copy-start = (bf16[1,128,4096]{2,1,0:T(8,128)(2,1)S(1)}, bf16[1,128,4096]{2,1,0:T(8,128)(2,1)}, u32[]{:S(2)}) copy-start(bf16[1,128,4096]{2,1,0:T(8,128)(2,1)} %param.15) | copy-start | bytes 3145732
  28.8 5.9 %collective-permute-start.2 = (bf16[16,32,128]{2,1,0:T(8,128)(2,1)S(1)}, bf16[16,32,128]{2,1,0:T(8,128)(2,1)S(1)}, u32[]{:S(2)}, u32[]{:S(2)}) collective-permute-start(bf16[16,32,128]{2,1,0:T(8,128)(2,1)S(1)} %all_to_all.10), channel_id=1, source_target_pairs={{112,368},{368,112},{128,384},{384,128},{144,400},{400,144},{160,4... | collective-permute-start | bytes 393224 | tf_op jit(solution)/shard_map/ppermute | solution.py:230
  29.5 5.4 %collective-permute-start.1 = (bf16[16,32,128]{2,1,0:T(8,128)(2,1)S(1)}, bf16[16,32,128]{2,1,0:T(8,128)(2,1)S(1)}, u32[]{:S(2)}, u32[]{:S(2)}) collective-permute-start(bf16[16,32,128]{2,1,0:T(8,128)(2,1)S(1)} %all_to_all.10), channel_id=1, source_target_pairs={{0,8},{8,0},{16,24},{24,16},{32,40},{40,32},{48,56},{56,48},{64,72... | collective-permute-start | bytes 393224 | tf_op jit(solution)/shard_map/ppermute | solution.py:231
  33.9 1.5 %collective-permute-start.3 = (bf16[128,4096]{1,0:T(8,128)(2,1)S(1)}, bf16[128,4096]{1,0:T(8,128)(2,1)S(1)}, u32[]{:S(2)}, u32[]{:S(2)}) collective-permute-start(bf16[128,4096]{1,0:T(8,128)(2,1)S(1)} %bitcast.30), channel_id=1, source_target_pairs={{112,120},{120,112},{128,136},{136,128},{144,152},{152,144},{160,1... | collective-permute-start | bytes 3145736 | tf_op jit(solution)/shard_map/ppermute | solution.py:232
